TPU v7x, 32 devices: a whole 2x2x4 slice. The times are simulated.
32 devices in a mesh: section: 4 (over x, core), tensor: 2 (over y), dp: 4 (over z).
Axes of the slice: x: 2, y: 2, z: 4, core: 2. Of those that a mesh axis runs over, the one named last changes fastest.
Arguments:
- hidden_in: bfloat16 [1, 512, 16384], P(None, 'dp', 'tensor'), may hold values from -6 to 6
- norm_gain: bfloat16 [4, 16384], P('section', 'tensor'), may hold values from 0.099609375 to 1.8984375
- trainer_kv: bfloat16 [4, 16384, 2048], P('section', ('tensor', 'dp')), may hold values from -0.046875 to 0.046875
- queries: bfloat16 [4, 1, 512, 16384], P('section', None, 'dp', 'tensor'), may hold values from -120 to 120
- kv_cache: bfloat16 [4, 1, 512, 16, 4096], P('section', None, 'dp', None, 'tensor'), may hold values from -4 to 4, as said below
- cache_lengths: int32 [1, 512], P(None, 'dp'), may hold values from 1 to 16, as said below
Outputs:
- rollout_kv: bfloat16 [4, 16384, 2048], P('section', None, 'tensor')
- section_out: bfloat16 [4, 1, 512, 16384], P('section', None, 'dp', 'tensor')
Inputs may be any that keep to these rules, and one draw needn't show every extreme that they name: `kv_cache`: the two copies c = 0 and c = 1 of each head's keys and values are equal. `cache_lengths`: valid cache positions of each row; in every aligned block of 128 rows one row has 16 and one has 1.
All inputs are finite; a program needn't handle non-finite values.
Results may differ from a plain program's by a relative error of at most 0.0035.
The roundings to bfloat16 on the way count: a program that leaves them out, or rounds other values in their place, can miss the bound.
Values may be sent and summed in bfloat16 or wider, within the bound.
No kernel may reach another device: no remote copies, remote signals or barrier semaphores. Data moves between devices by JAX's collectives and lax.ppermute only.
A program may use at most 384 MiB of HBM per device.

v0:
```python
import functools

import jax
import jax.numpy as jnp
from jax import lax
from jax.experimental import pallas as pl
from jax.experimental.pallas import tpu as pltpu
from jax.sharding import PartitionSpec as P

D = 16384
KVH = 8
HD = 128
GQ = 16
GROUP = 128
LMAX = 16
HALF = GQ // 2
PAIR = 2 * HD
ROW_TILE = 16

epsilon = 1e-05
clip_ratio = 2.0
VMEM = 60 << 20
SHORT = pl.CostEstimate(flops=0, bytes_accessed=0, transcendentals=0)


def requantize_kernel(column_ref, w_ref, *o_refs):
    width = o_refs[0].shape[1]
    for j, o_ref in enumerate(o_refs):
        columns = pl.ds(pl.multiple_of(column_ref[j], HD), width)
        for start in range(0, w_ref.shape[0], GROUP):
            block = w_ref[start : start + GROUP, columns].astype(jnp.float32)
            limit = clip_ratio * (jnp.sum(jnp.abs(block), axis=0, keepdims=True) * (1.0 / GROUP))
            o_ref[start : start + GROUP, :] = jnp.clip(block, -limit, limit).astype(jnp.bfloat16)


def requantize(weight, columns, width):
    rows, whole = weight.shape
    tile = min(rows, 2 * GROUP)
    return pl.pallas_call(
        requantize_kernel,
        out_shape=[jax.ShapeDtypeStruct((rows, width), jnp.bfloat16)] * len(columns),
        grid_spec=pltpu.PrefetchScalarGridSpec(
            num_scalar_prefetch=1,
            grid=(rows // tile,),
            in_specs=[pl.BlockSpec((tile, whole), lambda i, columns: (i, 0))],
            out_specs=[pl.BlockSpec((tile, width), lambda i, columns: (i, 0))] * len(columns),
        ),
        compiler_params=pltpu.CompilerParams(vmem_limit_bytes=VMEM),
        cost_estimate=SHORT,
    )(jnp.stack(columns), weight)


def project_kernel(layout, lhs_count, has_total, has_held, placed, where_ref, *refs):
    lhs = refs[:lhs_count]
    blocks = refs[lhs_count : lhs_count + len(layout)]
    rest = list(refs[lhs_count + len(layout) :])
    total = rest.pop(0)[...] if has_total else None
    if has_held:
        rest.pop(0)
    o_ref = rest.pop(0)
    segments = [(block, *segment) for block, of_block in zip(blocks, layout) for segment in of_block]

    def copies():
        out, sems = rest
        width = min(out.shape[1], o_ref.shape[1])
        for i, (block, _, start, depth) in enumerate(segments):
            rows = pl.ds(pl.multiple_of(where_ref[2 + 2 * i + 1], GROUP), depth)
            columns = pl.ds(pl.multiple_of(pl.program_id(0) * width, HD), width)
            source = block.at[pl.ds(start, depth)]
            if width < block.shape[1]:
                source = block.at[pl.ds(start, depth), pl.ds(pl.multiple_of(where_ref[1], HD), width)]
            yield pltpu.make_async_copy(source, out.at[rows, columns], sems.at[i])

    if placed:

        @pl.when(where_ref[0] == 1)
        def _():
            for copy in copies():
                copy.start()

    for i, (block, j, start, depth) in enumerate(segments):
        columns = pl.ds(pl.multiple_of(where_ref[2 + 2 * i], GROUP), depth)
        term = jnp.dot(lhs[j][:, columns], block[start : start + depth, :], preferred_element_type=jnp.float32)
        total = term if total is None else total + term
    o_ref[...] = total

    if placed:

        @pl.when(where_ref[0] == 1)
        def _():
            for copy in copies():
                copy.wait()


def project(lhs, terms, total=None, placing=None, rollout=None):
    rows = lhs[0].shape[0]
    served = terms[0][0].shape[1]
    tile = min(served, 256)
    active, first_column, width = placing or (0, 0, 0)
    where = [active, first_column]
    for _, segments in terms:
        for _, offset, row, _, _ in segments:
            where += [offset, row]
    layout = [[(j, start, depth) for j, _, _, start, depth in segments] for _, segments in terms]
    count = sum(len(segments) for segments in layout)
    added = () if total is None else (total,)
    held = () if rollout is None else (rollout,)
    column = lambda i, where: (0, i)
    anywhere = pl.BlockSpec(memory_space=pl.ANY)
    fresh_shape, fresh_spec = jax.ShapeDtypeStruct((rows, served), jnp.float32), pl.BlockSpec((rows, tile), column)
    return pl.pallas_call(
        functools.partial(project_kernel, layout, len(lhs), bool(added), bool(held), placing is not None),
        out_shape=[fresh_shape, jax.ShapeDtypeStruct((D, width), jnp.bfloat16)] if placing else fresh_shape,
        grid_spec=pltpu.PrefetchScalarGridSpec(
            num_scalar_prefetch=1,
            grid=(served // tile,),
            in_specs=[pl.BlockSpec(part.shape, lambda i, where: (0, 0)) for part in lhs]
            + [pl.BlockSpec((block.shape[0], tile), column) for block, _ in terms]
            + [fresh_spec for _ in added]
            + [anywhere for _ in held],
            out_specs=[fresh_spec, anywhere] if placing else fresh_spec,
            scratch_shapes=[pltpu.SemaphoreType.DMA((count,))] if placing else [],
        ),
        input_output_aliases={1 + len(lhs) + len(terms) + len(added): 1} if held else {},
        compiler_params=pltpu.CompilerParams(vmem_limit_bytes=VMEM),
        cost_estimate=SHORT,
    )(jnp.stack([jnp.asarray(v, jnp.int32) for v in where]), *lhs, *[block for block, _ in terms], *added, *held)


def attend_kernel(share, bias_ref, x_ref, q_ref, c_ref, f_ref, o_ref):
    heads = share * HALF
    bias = bias_ref[0]
    scale = HD ** (-0.5)
    for g in range(q_ref.shape[1] // (heads * HD)):
        lanes = [slice((g * heads + i) * HD, (g * heads + i + 1) * HD) for i in range(heads)]
        query = jnp.concatenate([q_ref[:, lane] for lane in lanes], axis=0)
        at = g * share * PAIR
        keys = c_ref[:, :, at : at + HD].reshape(ROW_TILE * LMAX, HD)
        values = c_ref[:, :, at + HD : at + PAIR].reshape(ROW_TILE * LMAX, HD)
        fresh = f_ref[:, g * PAIR : (g + 1) * PAIR].astype(jnp.bfloat16).astype(jnp.float32)
        new_key = jnp.concatenate([fresh[:, :HD]] * heads, axis=0)
        new_value = jnp.concatenate([fresh[:, HD:]] * heads, axis=0)
        old = lax.dot_general(query, keys, (((1,), (1,)), ((), ())), preferred_element_type=jnp.float32)
        old = old * scale + bias
        new = jnp.sum(query.astype(jnp.float32) * new_key, axis=1, keepdims=True) * scale
        highest = jnp.maximum(jnp.max(old, axis=1, keepdims=True), new)
        old = jnp.exp(old - highest)
        new = jnp.exp(new - highest)
        inverse = 1.0 / (jnp.sum(old, axis=1, keepdims=True) + new)
        old = (old * inverse).astype(jnp.bfloat16)
        new = (new * inverse).astype(jnp.bfloat16).astype(jnp.float32)
        mixed = jnp.dot(old, values, preferred_element_type=jnp.float32) + new * new_value
        for i, lane in enumerate(lanes):
            total = x_ref[:, lane].astype(jnp.float32) + mixed[i * ROW_TILE : (i + 1) * ROW_TILE, :]
            o_ref[:, lane] = total.astype(jnp.bfloat16)


def seen_bias(lengths, heads):
    owner = jnp.arange(ROW_TILE)
    own = (owner[:, None, None] == owner[None, :, None]) & jnp.ones((1, 1, LMAX), bool)
    seen = jnp.arange(LMAX)[None, None, None, :] < lengths.reshape(-1, ROW_TILE, 1, 1)
    bias = jnp.where(own[None] & seen, 0.0, -jnp.inf).astype(jnp.float32)
    bias = jnp.broadcast_to(bias[:, None], (bias.shape[0], heads, ROW_TILE, ROW_TILE, LMAX))
    return bias.reshape(-1, heads * ROW_TILE, ROW_TILE * LMAX)


def attend(current, query, cache, bias, fresh):
    rows, width = query.shape
    share = min(2, width // (HALF * HD))
    wide = pl.BlockSpec((ROW_TILE, width), lambda i: (i, 0))
    return pl.pallas_call(
        functools.partial(attend_kernel, share),
        out_shape=jax.ShapeDtypeStruct((rows, width), jnp.bfloat16),
        grid=(rows // ROW_TILE,),
        in_specs=[
            pl.BlockSpec((1, *bias.shape[1:]), lambda i: (i, 0, 0)),
            wide,
            wide,
            pl.BlockSpec((ROW_TILE, LMAX, cache.shape[2]), lambda i: (i, 0, 0)),
            pl.BlockSpec((ROW_TILE, fresh.shape[1]), lambda i: (i, 0)),
        ],
        out_specs=wide,
        compiler_params=pltpu.CompilerParams(vmem_limit_bytes=VMEM),
        cost_estimate=SHORT,
    )(bias, current, query, cache, fresh)


def together(*values):
    return lax.optimization_barrier(values)


def body(hidden_in, norm_gain, trainer_kv, queries, kv_cache, cache_lengths):
    sections, tensors, dps = (lax.axis_size(axis) for axis in ("section", "tensor", "dp"))
    section, tensor, dp = (lax.axis_index(axis) for axis in ("section", "tensor", "dp"))
    rows = hidden_in.shape[1]
    depth = trainer_kv.shape[1]
    own_width = 2 * KVH * HD // tensors
    served = max(own_width, PAIR)
    early, late = (1, 2), (0, 3)
    everyone = tuple(range(sections))
    is_early = ((section == 1) | (section == 2)).astype(jnp.int32)
    inner = (dp == 1) | (dp == 2)

    def over(axis, count, value, routes):
        pairs = [(a * count + i, b * count + j) for a, b, i, j in routes]
        return lax.ppermute(value, ("section", axis), pairs)

    def over_dp(value, at, target):
        return over("dp", dps, value, [(s, s, z, target[z]) for s in at for z in range(dps)])

    def over_tensor(value, at, flip, step=0):
        return over("tensor", tensors, value, [(s, s + step, t, t ^ flip) for s in at for t in range(tensors)])

    def flipped(b):
        return [z ^ b for z in range(dps)]

    def feature_block(value, b):
        return lax.dynamic_slice_in_dim(value, (dp ^ b) * depth, depth, 1)

    def normed_of(parts, inverse, gains):
        return [
            (part.astype(jnp.float32) * inverse[:, None] * gain.astype(jnp.float32)).astype(jnp.bfloat16)
            for part, gain in zip(parts, gains)
        ]

    def square_sum(part):
        wide = part.astype(jnp.float32)
        return jnp.sum(wide * wide, axis=1)

    bias = seen_bias(cache_lengths[0], min(2, hidden_in.shape[2] // (HALF * HD)) * HALF)

    def attended(current, fresh):
        return attend(current, queries[0, 0], kv_cache[0, 0], bias, fresh)

    def hop(value, tick):
        return [over_tensor(value, (tick - 1,), j, 1) for j in range(tensors)]

    def prepared(parts):
        inverse = lax.rsqrt(sum(square_sum(part) for part in parts) / D + epsilon)
        return normed_of(parts, inverse, gains)

    halves = [[(0, 0)], [(j, (j - 1) * depth) for j in range(1, tensors)]]

    def straight(at, block):
        return {0: block, 3: over_dp(block, at, flipped(3)), 1: over_dp(block, at, flipped(1))}

    def relayed(at, blocks):
        return over_dp(jnp.where(inner, blocks[3], blocks[0]), at, (2, 0, 3, 1))

    def terms_of(half, blocks, which, shift=0):
        return [
            (
                blocks[b],
                [
                    (j, (dp ^ b) * depth + shift, ((tensor ^ j) * dps + (dp ^ b)) * depth, start, depth)
                    for j, start in halves[half]
                ],
            )
            for b in which
        ]

    def placing(active):
        return (active, tensor * own_width % served, own_width)

    kept = requantize(trainer_kv[0], [(tensor ^ j) * own_width // served * served for j in range(tensors)], served)
    hidden, kept = together(hidden_in[0], kept)

    squares = square_sum(hidden)
    for j in (2**i for i in range(tensors.bit_length() - 1)):
        squares = squares + over_tensor(squares, (0,), j)
    (normed,) = normed_of([hidden], lax.rsqrt(squares / D + epsilon), [norm_gain])
    first = [feature_block(normed, b) for b in range(dps)]
    first[1:] = [over_dp(first[b], (0,), flipped(b)) for b in range(1, dps)]
    gains = [norm_gain] + [over_tensor(norm_gain, everyone, j) for j in range(1, tensors)]

    def others(at, kept):
        received = [over_tensor(kept[j], at, j) for j in range(1, tensors)]
        return received[0] if len(received) == 1 else jnp.concatenate(received, axis=0)

    early_own = straight(early, kept[0])

    lhs = [jnp.concatenate(first, axis=0)]
    partial = [project(lhs, [(kept[j], [(0, 0, 0, 0, depth)])]) for j in range(tensors)]
    partial, kept = together(partial, kept)
    early_rest = others(early, kept)
    total = partial[0]
    for j in range(1, tensors):
        total = total + over_tensor(partial[j], (0,), j)
    total = total.reshape(dps, rows, served)
    returned = [over_dp(total[b].astype(jnp.bfloat16), (0,), flipped(b)) for b in range(1, dps)]
    fresh = total[0]
    for part in returned:
        fresh = fresh + part.astype(jnp.float32)
    result = carried = attended(hidden, fresh)

    early_other = straight(early, early_rest)
    early_own, carried, kept = together(early_own, carried, kept)
    early_own[2] = relayed(early, early_own)
    moved = hop(carried, 1)
    late_rest = others(late, kept)

    early_own, early_other, late_rest = together(early_own, early_other, late_rest)
    early_other[2] = relayed(early, early_other)
    token = over("dp", dps, early_other[3][:ROW_TILE, :HD], [(a, b, z, z) for a, b in ((1, 0), (2, 3)) for z in range(dps)])
    token, late_block = together(token, kept[0])
    shift = jnp.isnan(token[0, 0]).astype(jnp.int32)
    late_own = straight(late, late_block)

    terms = terms_of(0, early_own, range(dps)) + terms_of(1, early_other, range(dps))
    fresh, rollout = project(prepared(moved), terms, None, placing(is_early))
    carried = attended(moved[0], fresh)
    result = jnp.where(section == 1, carried, result)

    late_rest, carried = together(late_rest, carried)
    late_other = straight(late, late_rest)
    moved = hop(carried, 2)
    late_own, moved = together(late_own, moved)
    late_own[2] = relayed(late, late_own)
    carried = attended(moved[0], project(prepared(moved), terms))
    result = jnp.where(section == 2, carried, result)
    moved = hop(carried, 3)

    normed = prepared(moved)
    late_other, late_own, normed, result = together(late_other, late_own, normed, result)
    late_other[2] = relayed(late, late_other)
    terms = terms_of(0, late_own, range(dps), shift) + terms_of(1, late_other, (0, 1, 3))
    fresh, rollout = project(normed, terms, None, placing(1 - is_early), rollout)
    fresh, rollout, last = together(fresh, rollout, late_other[2])
    fresh, rollout = project(normed, terms_of(1, {2: last}, (2,)), fresh, placing(1 - is_early), rollout)
    result = jnp.where(section == 3, attended(moved[0], fresh), result)
    return (rollout[None], result[None, None])


def solution(mesh):
    placed = (
        P(None, "dp", "tensor"),
        P("section", "tensor"),
        P("section", ("tensor", "dp"), None),
        P("section", None, "dp", "tensor"),
        P("section", None, "dp", None, "tensor"),
        P(None, "dp"),
    )
    return jax.shard_map(
        body,
        mesh=mesh,
        in_specs=placed,
        out_specs=(P("section", None, "tensor"), P("section", None, "dp", "tensor")),
        check_vma=False,
    )
```

profile of v0, /device:TPU:0, one launch (start us, length us, event | category | flops | bytes accessed | tf_op | source)
XLA Modules:
  0.0 662.7 jit_solution(3789037391877339841)
XLA Ops:
  1.3 10.8 %shard_map.77 = (bf16[2048,1024]{1,0:T(8,128)(2,1)}, bf16[2048,1024]{1,0:T(8,128)(2,1)}) custom-call(s32[2]{0:T(128)} %pad_add_fusion.1.column_ref, bf16[2048,2048]{1,0:T(8,128)(2,1)} %bitcast.45), custom_call_target="tpu_custom_call" | custom-call | tf_op jit(solution)/shard_map/pallas_call | solution.py:39
  12.6 4.9 collective-permute-start.2
  17.6 1.4 collective-permute-done.2
  19.9 6.0 collective-permute-start.5
  25.9 1.9 collective-permute-start.4
  27.9 2.5 collective-permute-start.3
  30.3 2.6 collective-permute-start.1
  33.0 2.7 collective-permute-start
  35.6 3.3 collective-permute-done.5
  38.9 64.2 %collective-permute-done.4 = bf16[128,2048]{1,0:T(8,128)(2,1)S(1)} collective-permute-done((bf16[128,2048]{1,0:T(8,128)(2,1)S(1)}, bf16[128,2048]{1,0:T(8,128)(2,1)S(1)}, u32[]{:S(2)}, u32[]{:S(2)}) %collective-permute-start.4) | collective-permute-done | bytes 524320 | tf_op jit(solution)/shard_map/ppermute | solution.py:206
  103.1 1.6 pad_maximum_fusion.refs_0_
  105.2 7.1 %shard_map.78 = f32[512,1024]{1,0:T(8,128)} custom-call(s32[4]{0:T(128)} %broadcast_5_where_ref.2.where_ref, bf16[512,2048]{1,0:T(8,128)(2,1)} %pad_maximum_fusion.refs_0_, bf16[2048,1024]{1,0:T(8,128)(2,1)} %get-tuple-element.88.refs_1_.refs_2_), custom_call_target="tpu_custom_call" | custom-call | tf_op jit(solution)/shard_map/pallas_call | solution.py:111
  112.2 7.3 %shard_map.79 = f32[512,1024]{1,0:T(8,128)} custom-call(s32[4]{0:T(128)} %broadcast_5_where_ref.2.where_ref, bf16[512,2048]{1,0:T(8,128)(2,1)} %pad_maximum_fusion.refs_0_, bf16[2048,1024]{1,0:T(8,128)(2,1)} %get-tuple-element.65.refs_1_), custom_call_target="tpu_custom_call" | custom-call | tf_op jit(solution)/shard_map/pallas_call | solution.py:111
  119.5 3.5 collective-permute-start.6
  123.0 2.7 collective-permute-start.11
  125.8 22.0 %collective-permute-done.6 = f32[512,1024]{1,0:T(8,128)S(1)} collective-permute-done((f32[512,1024]{1,0:T(8,128)}, f32[512,1024]{1,0:T(8,128)S(1)}, u32[]{:S(2)}, u32[]{:S(2)}) %collective-permute-start.6) | collective-permute-done | bytes 2097184 | tf_op jit(solution)/shard_map/ppermute | solution.py:206
  147.7 1.9 fusion.23
  149.7 2.6 collective-permute-start.7
  153.7 4.7 collective-permute-start.9
  158.4 2.4 collective-permute-done.7
  160.8 4.0 collective-permute-start.8
  165.0 8.3 %broadcast_in_dim.16 = f32[8,16,16,16,16]{4,3,2,1,0:T(8,128)} broadcast(f32[8,16,16,16]{3,2,1,0:T(8,128)S(1)} %and_select_fusion), dimensions={0,2,3,4} | broadcast | bytes 2228224 | tf_op jit(solution)/shard_map/broadcast_in_dim | solution.py:163
  173.3 12.5 %reshape.69.bias_ref = f32[8,256,256]{2,1,0:T(8,128)} reshape(f32[8,16,16,16,16]{4,3,2,1,0:T(8,128)} %broadcast_in_dim.16) | data formatting | bytes 4194304 | tf_op jit(solution)/shard_map/reshape | solution.py:164
  185.8 66.8 %collective-permute-done.8 = bf16[128,1024]{1,0:T(8,128)(2,1)S(1)} collective-permute-done((bf16[128,1024]{1,0:T(8,128)(2,1)S(1)}, bf16[128,1024]{1,0:T(8,128)(2,1)S(1)}, u32[]{:S(2)}, u32[]{:S(2)}) %collective-permute-start.8) | collective-permute-done | bytes 262176 | tf_op jit(solution)/shard_map/ppermute | solution.py:206
  252.6 2.0 fusion.22.f_ref
  254.6 12.6 %shard_map.80 = bf16[128,8192]{1,0:T(8,128)(2,1)} custom-call(f32[8,256,256]{2,1,0:T(8,128)} %reshape.69.bias_ref, bf16[128,8192]{1,0:T(8,128)(2,1)} %bitcast.42, bf16[128,8192]{1,0:T(8,128)(2,1)} %bitcast.38, bf16[128,16,2048]{2,1,0:T(8,128)(2,1)} %bitcast.34, f32[128,1024]{1,0:T(8,128)} %fusion.22.f_ref), custom_call_target="tpu_custom_call" | custom-call | tf_op jit(solution)/shard_map/pallas_call | solution.py:171
  267.2 2.6 broadcast_select_fusion.3
  270.8 3.4 collective-permute-start.14
  276.1 2.7 collective-permute-start.16
  278.8 1.6 collective-permute-start.15
  280.4 41.4 %collective-permute-done.14.refs_6_ = bf16[2048,1024]{1,0:T(8,128)(2,1)S(1)} collective-permute-done((bf16[2048,1024]{1,0:T(8,128)(2,1)}, bf16[2048,1024]{1,0:T(8,128)(2,1)S(1)}, u32[]{:S(2)}, u32[]{:S(2)}) %collective-permute-start.14) | collective-permute-done | bytes 4194336 | tf_op jit(solution)/shard_map/ppermute | solution.py:206
  321.8 7.8 %broadcast_select_fusion.2 = bf16[2048,1024]{1,0:T(8,128)(2,1)} fusion(bf16[2048,1024]{1,0:T(8,128)(2,1)S(1)} %collective-permute-done.13.refs_9_, bf16[2048,1024]{1,0:T(8,128)(2,1)} %collective-permute-done.11.refs_6_, pred[]{:T(512)S(6)} %or.7), kind=kLoop, calls=%fused_computation.37 | loop fusion | flops 2097152 | bytes 12582913 | tf_op jit(solution)/shard_map/jit(_where)/select_n | solution.py:248
  329.6 2.6 collective-permute-start.18
  332.3 1.5 collective-permute-start.17
  334.4 10.2 %collective-permute-done.17 = bf16[1,8192]{1,0:T(2,128)(2,1)S(1)} collective-permute-done((bf16[1,8192]{1,0:T(2,128)(2,1)S(1)}, bf16[1,8192]{1,0:T(2,128)(2,1)S(1)}, u32[]{:S(2)}, u32[]{:S(2)}) %collective-permute-start.17) | collective-permute-done | bytes 16416 | tf_op jit(solution)/shard_map/ppermute | solution.py:206
  344.7 2.1 fusion.6
  347.4 1.3 collective-permute-start.21
  349.2 1.3 collective-permute-done.21
  350.5 5.3 collective-permute-start.23
  355.8 1.9 collective-permute-start.22
  357.7 4.7 fusion.8
  362.4 16.1 %shard_map.81 = (f32[128,1024]{1,0:T(8,128)}, bf16[16384,1024]{1,0:T(8,128)(2,1)}) custom-call(s32[18]{0:T(128)} %stack.132.where_ref, bf16[128,8192]{1,0:T(8,128)(2,1)} %get-tuple-element.118.refs_0_, bf16[128,8192]{1,0:T(8,128)(2,1)} %get-tuple-element.117.refs_1_, bf16[2048,1024]{1,0:T(8,128)(2,1)} %get-tuple-element.88.refs_1_.refs_2_, ...), custom_call_target="tpu_custom_call" | custom-call | tf_op jit(solution)/shard_map/pallas_call | solution.py:111
  378.5 12.6 %shard_map.82 = bf16[128,8192]{1,0:T(8,128)(2,1)} custom-call(f32[8,256,256]{2,1,0:T(8,128)} %reshape.69.bias_ref, bf16[128,8192]{1,0:T(8,128)(2,1)} %copy-done.3, bf16[128,8192]{1,0:T(8,128)(2,1)} %bitcast.39, bf16[128,16,2048]{2,1,0:T(8,128)(2,1)} %bitcast.35, f32[128,1024]{1,0:T(8,128)} %get-tuple-element.75.f_ref), custom_call_target="tpu_custom_call" | custom-call | tf_op jit(solution)/shard_map/pallas_call | solution.py:171
  391.2 2.0 collective-permute-start.25
  394.6 2.3 collective-permute-start.20
  397.0 6.2 collective-permute-done.23.refs_5_
  403.2 45.4 %collective-permute-start.19 = (bf16[2048,1024]{1,0:T(8,128)(2,1)}, bf16[2048,1024]{1,0:T(8,128)(2,1)}, u32[]{:S(2)}, u32[]{:S(2)}) collective-permute-start(bf16[2048,1024]{1,0:T(8,128)(2,1)} %copy-done.7), channel_id=1, source_target_pairs={{0,1},{1,0},{2,3},{3,2},{24,25},{25,24},{26,27},{27,26},{4,5},{5,4... | collective-permute-start | bytes 12582920 | tf_op jit(solution)/shard_map/ppermute | solution.py:206
  448.6 3.3 fusion.9
  451.9 4.8 fusion.14
  456.7 16.0 %shard_map.83.f_ref = f32[128,1024]{1,0:T(8,128)} custom-call(s32[18]{0:T(128)} %stack.133.where_ref, bf16[128,8192]{1,0:T(8,128)(2,1)} %get-tuple-element.116.refs_0_, bf16[128,8192]{1,0:T(8,128)(2,1)} %get-tuple-element.115.refs_1_, bf16[2048,1024]{1,0:T(8,128)(2,1)} %get-tuple-element.88.refs_1_.refs_2_, bf16[2048,1024]{1,0:T(8,128)(2,1)} %collective-permute-done.refs_3_, ...), custom_call_target="tpu_custom_call" | custom-call | tf_op jit(solution)/shard_map/pallas_call | solution.py:111
  472.7 12.6 %shard_map.84 = bf16[128,8192]{1,0:T(8,128)(2,1)} custom-call(f32[8,256,256]{2,1,0:T(8,128)} %reshape.69.bias_ref, bf16[128,8192]{1,0:T(8,128)(2,1)} %copy-done.2, bf16[128,8192]{1,0:T(8,128)(2,1)} %bitcast.40, bf16[128,16,2048]{2,1,0:T(8,128)(2,1)} %bitcast.36, f32[128,1024]{1,0:T(8,128)} %shard_map.83.f_ref), custom_call_target="tpu_custom_call" | custom-call | tf_op jit(solution)/shard_map/pallas_call | solution.py:171
  487.2 2.6 broadcast_select_fusion.1
  489.9 3.2 collective-permute-start.26
  493.1 2.1 select_select_fusion
  496.2 3.1 fusion.20
  499.4 38.6 %collective-permute-done.19.refs_7_ = bf16[2048,1024]{1,0:T(8,128)(2,1)} collective-permute-done((bf16[2048,1024]{1,0:T(8,128)(2,1)}, bf16[2048,1024]{1,0:T(8,128)(2,1)}, u32[]{:S(2)}, u32[]{:S(2)}) %collective-permute-start.19) | collective-permute-done | bytes 4194336 | tf_op jit(solution)/shard_map/ppermute | solution.py:206
  538.0 44.8 %collective-permute-done.26.refs_4_ = bf16[2048,1024]{1,0:T(8,128)(2,1)S(1)} collective-permute-done((bf16[2048,1024]{1,0:T(8,128)(2,1)S(1)}, bf16[2048,1024]{1,0:T(8,128)(2,1)S(1)}, u32[]{:S(2)}, u32[]{:S(2)}) %collective-permute-start.26) | collective-permute-done | bytes 4194336 | tf_op jit(solution)/shard_map/ppermute | solution.py:206
  582.8 2.7 broadcast_select_fusion
  586.1 7.2 %collective-permute-start.29 = (bf16[2048,1024]{1,0:T(8,128)(2,1)}, bf16[2048,1024]{1,0:T(8,128)(2,1)}, u32[]{:S(2)}, u32[]{:S(2)}) collective-permute-start(bf16[2048,1024]{1,0:T(8,128)(2,1)} %broadcast_select_fusion), channel_id=1, source_target_pairs={{0,2},{1,0},{2,3},{3,1},{24,26},{25,24},{26,27},{27,25},{4,6},{5,4... | collective-permute-start | bytes 12582920 | tf_op jit(solution)/shard_map/ppermute | solution.py:206
  596.4 24.6 %shard_map.85 = (f32[128,1024]{1,0:T(8,128)}, bf16[16384,1024]{1,0:T(8,128)(2,1)}) custom-call(s32[16]{0:T(128)} %stack.138.where_ref, bf16[128,8192]{1,0:T(8,128)(2,1)} %get-tuple-element.85.refs_0_, bf16[128,8192]{1,0:T(8,128)(2,1)} %get-tuple-element.86.refs_1_, ...), custom_call_target="tpu_custom_call", output_to_operand_aliasing={{1}: (10, {})} | custom-call | tf_op jit(solution)/shard_map/pallas_call | solution.py:111
  621.0 18.6 %collective-permute-done.29.refs_2_ = bf16[2048,1024]{1,0:T(8,128)(2,1)} collective-permute-done((bf16[2048,1024]{1,0:T(8,128)(2,1)}, bf16[2048,1024]{1,0:T(8,128)(2,1)}, u32[]{:S(2)}, u32[]{:S(2)}) %collective-permute-start.29) | collective-permute-done | bytes 4194336 | tf_op jit(solution)/shard_map/ppermute | solution.py:206
  639.6 8.9 %shard_map.86 = (f32[128,1024]{1,0:T(8,128)}, bf16[16384,1024]{1,0:T(8,128)(2,1)}) custom-call(s32[4]{0:T(128)} %pad_add_fusion.where_ref, bf16[128,8192]{1,0:T(8,128)(2,1)} %get-tuple-element.85.refs_0_, bf16[128,8192]{1,0:T(8,128)(2,1)} %get-tuple-element.86.refs_1_, ...), custom_call_target="tpu_custom_call", output_to_operand_aliasing={{1}: (5, {})} | custom-call | tf_op jit(solution)/shard_map/pallas_call | solution.py:111
  648.5 12.6 %shard_map.87 = bf16[128,8192]{1,0:T(8,128)(2,1)} custom-call(f32[8,256,256]{2,1,0:T(8,128)} %reshape.69.bias_ref, bf16[128,8192]{1,0:T(8,128)(2,1)} %copy-done.4, bf16[128,8192]{1,0:T(8,128)(2,1)} %bitcast.41, bf16[128,16,2048]{2,1,0:T(8,128)(2,1)} %bitcast.37, f32[128,1024]{1,0:T(8,128)} %get-tuple-element.102.f_ref), custom_call_target="tpu_custom_call" | custom-call | tf_op jit(solution)/shard_map/pallas_call | solution.py:171
  661.2 1.5 select_bitcast_fusion
  (81 shorter events, 15.6 us)
Async XLA Ops:
  1.3 10.8 %copy-start.1 = (bf16[1,128,8192]{2,1,0:T(8,128)(2,1)S(1)}, bf16[1,128,8192]{2,1,0:T(8,128)(2,1)}, u32[]{:S(2)}) copy-start(bf16[1,128,8192]{2,1,0:T(8,128)(2,1)} %param.6) | copy-start | bytes 6291460
  1.3 16.2 %copy-start.13 = (bf16[1,8192]{1,0:T(2,128)(2,1)S(1)}, bf16[1,8192]{1,0:T(2,128)(2,1)}, u32[]{:S(2)}) copy-start(bf16[1,8192]{1,0:T(2,128)(2,1)} %param.7) | copy-start | bytes 49156
  12.6 6.4 collective-permute-start.2
  19.9 19.0 %collective-permute-start.5 = (bf16[128,2048]{1,0:T(8,128)(2,1)S(1)}, bf16[128,2048]{1,0:T(8,128)(2,1)S(1)}, u32[]{:S(2)}, u32[]{:S(2)}) collective-permute-start(bf16[128,2048]{1,0:T(8,128)(2,1)S(1)} %get-tuple-element.107), channel_id=1, source_target_pairs={{0,3},{1,2},{2,1},{3,0},{4,7},{5,6},{6,5},{7,4}} | collective-permute-start | bytes 1572872 | tf_op jit(solution)/shard_map/ppermute | solution.py:206
  25.9 77.1 %collective-permute-start.4 = (bf16[128,2048]{1,0:T(8,128)(2,1)S(1)}, bf16[128,2048]{1,0:T(8,128)(2,1)S(1)}, u32[]{:S(2)}, u32[]{:S(2)}) collective-permute-start(bf16[128,2048]{1,0:T(8,128)(2,1)S(1)} %get-tuple-element.108), channel_id=1, source_target_pairs={{0,2},{1,3},{2,0},{3,1},{4,6},{5,7},{6,4},{7,5}} | collective-permute-start | bytes 1572872 | tf_op jit(solution)/shard_map/ppermute | solution.py:206
  27.9 75.2 %collective-permute-start.3 = (bf16[128,2048]{1,0:T(8,128)(2,1)S(1)}, bf16[128,2048]{1,0:T(8,128)(2,1)S(1)}, u32[]{:S(2)}, u32[]{:S(2)}) collective-permute-start(bf16[128,2048]{1,0:T(8,128)(2,1)S(1)} %get-tuple-element.109), channel_id=1, source_target_pairs={{0,1},{1,0},{2,3},{3,2},{4,5},{5,4},{6,7},{7,6}} | collective-permute-start | bytes 1572872 | tf_op jit(solution)/shard_map/ppermute | solution.py:206
  30.3 236.9 %collective-permute-start.1 = (bf16[2048,1024]{1,0:T(8,128)(2,1)}, bf16[2048,1024]{1,0:T(8,128)(2,1)}, u32[]{:S(2)}, u32[]{:S(2)}) collective-permute-start(bf16[2048,1024]{1,0:T(8,128)(2,1)} %get-tuple-element.88.refs_1_.refs_2_), channel_id=1, source_target_pairs={{8,11},{9,10},{10,9},{11,8},{16,19},{17,18},{18,17},{19,16},{12,15... | collective-permute-start | bytes 12582920 | tf_op jit(solution)/shard_map/ppermute | solution.py:206
  33.0 234.3 %collective-permute-start = (bf16[2048,1024]{1,0:T(8,128)(2,1)}, bf16[2048,1024]{1,0:T(8,128)(2,1)}, u32[]{:S(2)}, u32[]{:S(2)}) collective-permute-start(bf16[2048,1024]{1,0:T(8,128)(2,1)} %get-tuple-element.88.refs_1_.refs_2_), channel_id=1, source_target_pairs={{8,9},{9,8},{10,11},{11,10},{16,17},{17,16},{18,19},{19,18},{12,13... | collective-permute-start | bytes 12582920 | tf_op jit(solution)/shard_map/ppermute | solution.py:206
  112.2 35.5 %copy-start.11 = (f32[512,1024]{1,0:T(8,128)S(1)}, f32[512,1024]{1,0:T(8,128)}, u32[]{:S(2)}) copy-start(f32[512,1024]{1,0:T(8,128)} %shard_map.78) | copy-start | bytes 6291460
  119.5 33.4 %copy-start.14 = (s32[1,128]{1,0:T(1,128)S(1)}, s32[1,128]{1,0:T(1,128)}, u32[]{:S(2)}) copy-start(s32[1,128]{1,0:T(1,128)} %param.11) | copy-start | bytes 1540
  119.5 28.3 %collective-permute-start.6 = (f32[512,1024]{1,0:T(8,128)}, f32[512,1024]{1,0:T(8,128)S(1)}, u32[]{:S(2)}, u32[]{:S(2)}) collective-permute-start(f32[512,1024]{1,0:T(8,128)} %shard_map.79), channel_id=1, source_target_pairs={{0,4},{4,0},{1,5},{5,1},{2,6},{6,2},{3,7},{7,3}} | collective-permute-start | bytes 6291464 | tf_op jit(solution)/shard_map/ppermute | solution.py:206
  123.0 151.2 %collective-permute-start.11 = (bf16[2048,1024]{1,0:T(8,128)(2,1)}, bf16[2048,1024]{1,0:T(8,128)(2,1)}, u32[]{:S(2)}, u32[]{:S(2)}) collective-permute-start(bf16[2048,1024]{1,0:T(8,128)(2,1)} %get-tuple-element.65.refs_1_), channel_id=1, source_target_pairs={{8,12},{12,8},{16,20},{20,16},{9,13},{13,9},{17,21},{21,17},{10,14... | collective-permute-start | bytes 12582920 | tf_op jit(solution)/shard_map/ppermute | solution.py:206
  149.7 11.1 %collective-permute-start.7 = (bf16[128,1024]{1,0:T(8,128)(2,1)S(1)}, bf16[128,1024]{1,0:T(8,128)(2,1)S(1)}, u32[]{:S(2)}, u32[]{:S(2)}) collective-permute-start(bf16[128,1024]{1,0:T(8,128)(2,1)S(1)} %get-tuple-element.110), channel_id=1, source_target_pairs={{0,1},{1,0},{2,3},{3,2},{4,5},{5,4},{6,7},{7,6}} | collective-permute-start | bytes 786440 | tf_op jit(solution)/shard_map/ppermute | solution.py:206
  153.7 32.1 %collective-permute-start.9 = (bf16[128,1024]{1,0:T(8,128)(2,1)S(1)}, bf16[128,1024]{1,0:T(8,128)(2,1)S(1)}, u32[]{:S(2)}, u32[]{:S(2)}) collective-permute-start(bf16[128,1024]{1,0:T(8,128)(2,1)S(1)} %get-tuple-element.111), channel_id=1, source_target_pairs={{0,3},{1,2},{2,1},{3,0},{4,7},{5,6},{6,5},{7,4}} | collective-permute-start | bytes 786440 | tf_op jit(solution)/shard_map/ppermute | solution.py:206
  160.8 91.8 %collective-permute-start.8 = (bf16[128,1024]{1,0:T(8,128)(2,1)S(1)}, bf16[128,1024]{1,0:T(8,128)(2,1)S(1)}, u32[]{:S(2)}, u32[]{:S(2)}) collective-permute-start(bf16[128,1024]{1,0:T(8,128)(2,1)S(1)} %get-tuple-element.112), channel_id=1, source_target_pairs={{0,2},{1,3},{2,0},{3,1},{4,6},{5,7},{6,4},{7,5}} | collective-permute-start | bytes 786440 | tf_op jit(solution)/shard_map/ppermute | solution.py:206
  269.9 8.9 %collective-permute-start.10 = (bf16[2048,1024]{1,0:T(8,128)(2,1)S(1)}, bf16[2048,1024]{1,0:T(8,128)(2,1)S(1)}, u32[]{:S(2)}, u32[]{:S(2)}) collective-permute-start(bf16[2048,1024]{1,0:T(8,128)(2,1)S(1)} %broadcast_select_fusion.3), channel_id=1, source_target_pairs={{8,10},{9,8},{10,11},{11,9},{16,18},{17,16},{18,19},{19,17},{12,14... | collective-permute-start | bytes 12582920 | tf_op jit(solution)/shard_map/ppermute | solution.py:206
  270.8 51.0 %collective-permute-start.14 = (bf16[2048,1024]{1,0:T(8,128)(2,1)}, bf16[2048,1024]{1,0:T(8,128)(2,1)S(1)}, u32[]{:S(2)}, u32[]{:S(2)}) collective-permute-start(bf16[2048,1024]{1,0:T(8,128)(2,1)} %get-tuple-element.65.refs_1_), channel_id=1, source_target_pairs={{0,4},{4,0},{24,28},{28,24},{1,5},{5,1},{25,29},{29,25},{2,6},{6,2... | collective-permute-start | bytes 12582920 | tf_op jit(solution)/shard_map/ppermute | solution.py:206
  274.3 47.5 %collective-permute-start.13 = (bf16[2048,1024]{1,0:T(8,128)(2,1)}, bf16[2048,1024]{1,0:T(8,128)(2,1)S(1)}, u32[]{:S(2)}, u32[]{:S(2)}) collective-permute-start(bf16[2048,1024]{1,0:T(8,128)(2,1)} %collective-permute-done.11.refs_6_), channel_id=1, source_target_pairs={{8,11},{9,10},{10,9},{11,8},{16,19},{17,18},{18,17},{19,16},{12,15... | collective-permute-start | bytes 12582920 | tf_op jit(solution)/shard_map/ppermute | solution.py:206
  275.2 46.6 %collective-permute-start.12 = (bf16[2048,1024]{1,0:T(8,128)(2,1)}, bf16[2048,1024]{1,0:T(8,128)(2,1)S(1)}, u32[]{:S(2)}, u32[]{:S(2)}) collective-permute-start(bf16[2048,1024]{1,0:T(8,128)(2,1)} %collective-permute-done.11.refs_6_), channel_id=1, source_target_pairs={{8,9},{9,8},{10,11},{11,10},{16,17},{17,16},{18,19},{19,18},{12,13... | collective-permute-start | bytes 12582920 | tf_op jit(solution)/shard_map/ppermute | solution.py:206
  276.1 68.5 %collective-permute-start.16 = (bf16[128,8192]{1,0:T(8,128)(2,1)}, bf16[128,8192]{1,0:T(8,128)(2,1)}, u32[]{:S(2)}, u32[]{:S(2)}) collective-permute-start(bf16[128,8192]{1,0:T(8,128)(2,1)} %shard_map.80), channel_id=1, source_target_pairs={{0,12},{4,8},{1,13},{5,9},{2,14},{6,10},{3,15},{7,11}} | collective-permute-start | bytes 6291464 | tf_op jit(solution)/shard_map/ppermute | solution.py:206
  278.8 43.0 %copy-start.5 = (bf16[2048,1024]{1,0:T(8,128)(2,1)}, bf16[2048,1024]{1,0:T(8,128)(2,1)S(1)}, u32[]{:S(2)}) copy-start(bf16[2048,1024]{1,0:T(8,128)(2,1)S(1)} %collective-permute-done.10.refs_4_) | copy-start | bytes 12582916
  278.8 69.9 %collective-permute-start.15 = (bf16[128,8192]{1,0:T(8,128)(2,1)}, bf16[128,8192]{1,0:T(8,128)(2,1)S(1)}, u32[]{:S(2)}, u32[]{:S(2)}) collective-permute-start(bf16[128,8192]{1,0:T(8,128)(2,1)} %shard_map.80), channel_id=1, source_target_pairs={{0,8},{4,12},{1,9},{5,13},{2,10},{6,14},{3,11},{7,15}} | collective-permute-start | bytes 6291464 | tf_op jit(solution)/shard_map/ppermute | solution.py:206
  321.8 7.9 %copy-start.7 = (bf16[2048,1024]{1,0:T(8,128)(2,1)}, bf16[2048,1024]{1,0:T(8,128)(2,1)S(1)}, u32[]{:S(2)}) copy-start(bf16[2048,1024]{1,0:T(8,128)(2,1)S(1)} %collective-permute-done.14.refs_6_) | copy-start | bytes 12582916
  321.8 7.8 %copy-start = (bf16[2048,1024]{1,0:T(8,128)(2,1)}, bf16[2048,1024]{1,0:T(8,128)(2,1)S(1)}, u32[]{:S(2)}) copy-start(bf16[2048,1024]{1,0:T(8,128)(2,1)S(1)} %collective-permute-done.13.refs_9_) | copy-start | bytes 12582916
  321.8 7.8 %copy-start.6 = (bf16[2048,1024]{1,0:T(8,128)(2,1)}, bf16[2048,1024]{1,0:T(8,128)(2,1)S(1)}, u32[]{:S(2)}) copy-start(bf16[2048,1024]{1,0:T(8,128)(2,1)S(1)} %collective-permute-done.12.refs_7_) | copy-start | bytes 12582916
  329.6 32.8 %collective-permute-start.18 = (bf16[2048,1024]{1,0:T(8,128)(2,1)}, bf16[2048,1024]{1,0:T(8,128)(2,1)}, u32[]{:S(2)}, u32[]{:S(2)}) collective-permute-start(bf16[2048,1024]{1,0:T(8,128)(2,1)} %broadcast_select_fusion.2), channel_id=1, source_target_pairs={{8,10},{9,8},{10,11},{11,9},{16,18},{17,16},{18,19},{19,17},{12,14... | collective-permute-start | bytes 12582920 | tf_op jit(solution)/shard_map/ppermute | solution.py:206
  332.3 12.3 %collective-permute-start.17 = (bf16[1,8192]{1,0:T(2,128)(2,1)S(1)}, bf16[1,8192]{1,0:T(2,128)(2,1)S(1)}, u32[]{:S(2)}, u32[]{:S(2)}) collective-permute-start(bf16[1,8192]{1,0:T(2,128)(2,1)S(1)} %copy-done.13), channel_id=1, source_target_pairs={{0,4},{4,0},{8,12},{12,8},{16,20},{20,16},{24,28},{28,24},{1,5},{5... | collective-permute-start | bytes 49160 | tf_op jit(solution)/shard_map/ppermute | solution.py:206
  347.4 3.0 collective-permute-start.21
  348.7 13.7 %copy-start.3 = (bf16[128,8192]{1,0:T(8,128)(2,1)}, bf16[128,8192]{1,0:T(8,128)(2,1)S(1)}, u32[]{:S(2)}) copy-start(bf16[128,8192]{1,0:T(8,128)(2,1)S(1)} %collective-permute-done.15.x_ref) | copy-start | bytes 6291460
  350.5 52.7 %collective-permute-start.23 = (bf16[2048,1024]{1,0:T(8,128)(2,1)}, bf16[2048,1024]{1,0:T(8,128)(2,1)}, u32[]{:S(2)}, u32[]{:S(2)}) collective-permute-start(bf16[2048,1024]{1,0:T(8,128)(2,1)} %get-tuple-element.88.refs_1_.refs_2_), channel_id=1, source_target_pairs={{0,3},{1,2},{2,1},{3,0},{24,27},{25,26},{26,25},{27,24},{4,7},{5,6... | collective-permute-start | bytes 12582920 | tf_op jit(solution)/shard_map/ppermute | solution.py:206
  355.8 92.8 %collective-permute-start.22 = (bf16[2048,1024]{1,0:T(8,128)(2,1)}, bf16[2048,1024]{1,0:T(8,128)(2,1)}, u32[]{:S(2)}, u32[]{:S(2)}) collective-permute-start(bf16[2048,1024]{1,0:T(8,128)(2,1)} %get-tuple-element.88.refs_1_.refs_2_), channel_id=1, source_target_pairs={{0,1},{1,0},{2,3},{3,2},{24,25},{25,24},{26,27},{27,26},{4,5},{5,4... | collective-permute-start | bytes 12582920 | tf_op jit(solution)/shard_map/ppermute | solution.py:206
  391.2 57.5 %collective-permute-start.25 = (bf16[128,8192]{1,0:T(8,128)(2,1)}, bf16[128,8192]{1,0:T(8,128)(2,1)}, u32[]{:S(2)}, u32[]{:S(2)}) collective-permute-start(bf16[128,8192]{1,0:T(8,128)(2,1)} %shard_map.82), channel_id=1, source_target_pairs={{8,20},{12,16},{9,21},{13,17},{10,22},{14,18},{11,23},{15,19}} | collective-permute-start | bytes 6291464 | tf_op jit(solution)/shard_map/ppermute | solution.py:206
  393.1 55.5 %collective-permute-start.24 = (bf16[128,8192]{1,0:T(8,128)(2,1)}, bf16[128,8192]{1,0:T(8,128)(2,1)S(1)}, u32[]{:S(2)}, u32[]{:S(2)}) collective-permute-start(bf16[128,8192]{1,0:T(8,128)(2,1)} %shard_map.82), channel_id=1, source_target_pairs={{8,16},{12,20},{9,17},{13,21},{10,18},{14,22},{11,19},{15,23}} | collective-permute-start | bytes 6291464 | tf_op jit(solution)/shard_map/ppermute | solution.py:206
  394.6 104.7 %collective-permute-start.20 = (bf16[2048,1024]{1,0:T(8,128)(2,1)}, bf16[2048,1024]{1,0:T(8,128)(2,1)}, u32[]{:S(2)}, u32[]{:S(2)}) collective-permute-start(bf16[2048,1024]{1,0:T(8,128)(2,1)} %copy-done.7), channel_id=1, source_target_pairs={{0,3},{1,2},{2,1},{3,0},{24,27},{25,26},{26,25},{27,24},{4,7},{5,6... | collective-permute-start | bytes 12582920 | tf_op jit(solution)/shard_map/ppermute | solution.py:206
  403.2 134.8 %collective-permute-start.19 = (bf16[2048,1024]{1,0:T(8,128)(2,1)}, bf16[2048,1024]{1,0:T(8,128)(2,1)}, u32[]{:S(2)}, u32[]{:S(2)}) collective-permute-start(bf16[2048,1024]{1,0:T(8,128)(2,1)} %copy-done.7), channel_id=1, source_target_pairs={{0,1},{1,0},{2,3},{3,2},{24,25},{25,24},{26,27},{27,26},{4,5},{5,4... | collective-permute-start | bytes 12582920 | tf_op jit(solution)/shard_map/ppermute | solution.py:206
  448.6 8.1 %copy-start.2 = (bf16[128,8192]{1,0:T(8,128)(2,1)}, bf16[128,8192]{1,0:T(8,128)(2,1)S(1)}, u32[]{:S(2)}) copy-start(bf16[128,8192]{1,0:T(8,128)(2,1)S(1)} %collective-permute-done.24.x_ref) | copy-start | bytes 6291460
  485.3 7.7 %copy-start.9 = (bf16[128,8192]{1,0:T(8,128)(2,1)S(1)}, bf16[128,8192]{1,0:T(8,128)(2,1)}, u32[]{:S(2)}) copy-start(bf16[128,8192]{1,0:T(8,128)(2,1)} %shard_map.82) | copy-start | bytes 6291460
  485.3 7.7 %copy-start.10 = (bf16[128,8192]{1,0:T(8,128)(2,1)S(1)}, bf16[128,8192]{1,0:T(8,128)(2,1)}, u32[]{:S(2)}) copy-start(bf16[128,8192]{1,0:T(8,128)(2,1)} %shard_map.84) | copy-start | bytes 6291460
  485.3 9.9 %collective-permute-start.28 = (bf16[128,8192]{1,0:T(8,128)(2,1)}, bf16[128,8192]{1,0:T(8,128)(2,1)S(1)}, u32[]{:S(2)}, u32[]{:S(2)}) collective-permute-start(bf16[128,8192]{1,0:T(8,128)(2,1)} %shard_map.84), channel_id=1, source_target_pairs={{16,28},{20,24},{17,29},{21,25},{18,30},{22,26},{19,31},{23,27}} | collective-permute-start | bytes 6291464 | tf_op jit(solution)/shard_map/ppermute | solution.py:206
  486.3 9.4 %collective-permute-start.27 = (bf16[128,8192]{1,0:T(8,128)(2,1)}, bf16[128,8192]{1,0:T(8,128)(2,1)S(1)}, u32[]{:S(2)}, u32[]{:S(2)}) collective-permute-start(bf16[128,8192]{1,0:T(8,128)(2,1)} %shard_map.84), channel_id=1, source_target_pairs={{16,24},{20,28},{17,25},{21,29},{18,26},{22,30},{19,27},{23,31}} | collective-permute-start | bytes 6291464 | tf_op jit(solution)/shard_map/ppermute | solution.py:206
  489.9 93.0 %collective-permute-start.26 = (bf16[2048,1024]{1,0:T(8,128)(2,1)S(1)}, bf16[2048,1024]{1,0:T(8,128)(2,1)S(1)}, u32[]{:S(2)}, u32[]{:S(2)}) collective-permute-start(bf16[2048,1024]{1,0:T(8,128)(2,1)S(1)} %broadcast_select_fusion.1), channel_id=1, source_target_pairs={{0,2},{1,0},{2,3},{3,1},{24,26},{25,24},{26,27},{27,25},{4,6},{5,4... | collective-permute-start | bytes 12582920 | tf_op jit(solution)/shard_map/ppermute | solution.py:206
  495.7 3.6 copy-start.4
  496.2 86.6 %copy-start.8 = (bf16[2048,1024]{1,0:T(8,128)(2,1)S(1)}, bf16[2048,1024]{1,0:T(8,128)(2,1)}, u32[]{:S(2)}) copy-start(bf16[2048,1024]{1,0:T(8,128)(2,1)} %copy-done.7) | copy-start | bytes 12582916
  582.8 3.3 copy-start.12
  586.1 53.5 %collective-permute-start.29 = (bf16[2048,1024]{1,0:T(8,128)(2,1)}, bf16[2048,1024]{1,0:T(8,128)(2,1)}, u32[]{:S(2)}, u32[]{:S(2)}) collective-permute-start(bf16[2048,1024]{1,0:T(8,128)(2,1)} %broadcast_select_fusion), channel_id=1, source_target_pairs={{0,2},{1,0},{2,3},{3,1},{24,26},{25,24},{26,27},{27,25},{4,6},{5,4... | collective-permute-start | bytes 12582920 | tf_op jit(solution)/shard_map/ppermute | solution.py:206
where the time goes:
time: 665 us; the launch traced here: 663 us
  waiting for transfers between devices  321 us (48%)
  Pallas kernels  141 us (21%)
  starting transfers between devices  124 us (19%)
  other arithmetic  47.8 us (7%)
  local copies, waits for them, and re-layouts  25.9 us (4%)
    ppermute x30, waiting for transfers between devices, over(): return lax.ppermute(value, ('section', axis), pairs)  321 us
    ppermute x30, starting transfers between devices, over(): return lax.ppermute(value, ('section', axis), pairs)  124 us
    pallas_call x6, Pallas kernels, project(): pl.pallas_call(functools.partial(project_kernel, layout, len(lhs), bool(a...  80 us
    pallas_call x4, Pallas kernels, attend(): pl.pallas_call(functools.partial(attend_kernel, share), out_shape=jax.Sha...  50.6 us
    select_n x4, other arithmetic, relayed(): return over_dp(jnp.where(inner, blocks[3], blocks[0]), at, (2, 0, 3, 1))  15.8 us
  transfers between devices with their start and end apart: 30, of which 13 were waited for; matrix products, arithmetic and copies ran while one was open for 10% of the time, Pallas kernels for 16%

commit v1 on v0

v1 whole, which is shorter than its diff:
```python
import functools

import jax
import jax.numpy as jnp
from jax import lax
from jax.experimental import pallas as pl
from jax.experimental.pallas import tpu as pltpu
from jax.sharding import PartitionSpec as P

D = 16384
KVH = 8
HD = 128
GQ = 16
GROUP = 128
LMAX = 16
HALF = GQ // 2
PAIR = 2 * HD
ROW_TILE = 16

epsilon = 1e-05
clip_ratio = 2.0
FIXED = 4
VMEM = 60 << 20
SHORT = pl.CostEstimate(flops=0, bytes_accessed=0, transcendentals=0)


def requantize_kernel(column_ref, w_ref, *o_refs):
    width = o_refs[0].shape[1]
    ones = jnp.ones((ROW_TILE, GROUP), jnp.bfloat16)
    for j, o_ref in enumerate(o_refs):
        columns = pl.ds(pl.multiple_of(column_ref[j], HD), width)
        for start in range(0, w_ref.shape[0], GROUP):
            block = w_ref[start : start + GROUP, columns]
            total = jnp.dot(ones, jnp.abs(block), preferred_element_type=jnp.float32)[:1]
            limit = (total * (clip_ratio / GROUP)).astype(jnp.bfloat16)
            o_ref[start : start + GROUP, :] = jnp.minimum(jnp.maximum(block, -limit), limit)


def requantize(weight, columns, width):
    rows, whole = weight.shape
    tile = min(rows, 2 * GROUP)
    return pl.pallas_call(
        requantize_kernel,
        out_shape=[jax.ShapeDtypeStruct((rows, width), jnp.bfloat16)] * len(columns),
        grid_spec=pltpu.PrefetchScalarGridSpec(
            num_scalar_prefetch=1,
            grid=(rows // tile,),
            in_specs=[pl.BlockSpec((tile, whole), lambda i, columns: (i, 0))],
            out_specs=[pl.BlockSpec((tile, width), lambda i, columns: (i, 0))] * len(columns),
        ),
        compiler_params=pltpu.CompilerParams(vmem_limit_bytes=VMEM),
        cost_estimate=SHORT,
    )(jnp.stack(columns), weight)


def project_kernel(layout, lhs_count, has_total, has_held, placed, where_ref, *refs):
    lhs = refs[:lhs_count]
    blocks = refs[lhs_count : lhs_count + len(layout)]
    rest = list(refs[lhs_count + len(layout) :])
    total_ref = rest.pop(0) if has_total else None
    if has_held:
        rest.pop(0)
    o_ref = rest.pop(0)
    segments = [(block, *segment) for block, of_block in zip(blocks, layout) for segment in of_block]

    def copies():
        out, sems = rest
        width = min(out.shape[1], o_ref.shape[1])
        for i, (block, _, start, depth) in enumerate(segments):
            rows = pl.ds(pl.multiple_of(where_ref[FIXED + 2 * i + 1], GROUP), depth)
            columns = pl.ds(pl.multiple_of(pl.program_id(0) * width, HD), width)
            source = block.at[pl.ds(start, depth)]
            if width < block.shape[1]:
                source = block.at[pl.ds(start, depth), pl.ds(pl.multiple_of(where_ref[2], HD), width)]
            yield pltpu.make_async_copy(source, out.at[rows, columns], sems.at[i])

    if placed:

        @pl.when(where_ref[1] == 1)
        def _():
            for copy in copies():
                copy.start()

    @pl.when(where_ref[0] == 1)
    def _():
        total = total_ref[...] if has_total else None
        for i, (block, j, start, depth) in enumerate(segments):
            columns = pl.ds(pl.multiple_of(where_ref[FIXED + 2 * i], GROUP), depth)
            term = jnp.dot(
                lhs[j][:, columns], block[start : start + depth, :], preferred_element_type=jnp.float32
            )
            total = term if total is None else total + term
        o_ref[...] = total

    @pl.when(where_ref[0] == 0)
    def _():
        o_ref[...] = jnp.zeros(o_ref.shape, jnp.float32)

    if placed:

        @pl.when(where_ref[1] == 1)
        def _():
            for copy in copies():
                copy.wait()


def project(active, lhs, terms, total=None, placing=None, rollout=None):
    used = sorted({segment[0] for _, segments in terms for segment in segments})
    lhs = [lhs[j] for j in used]
    rows = lhs[0].shape[0]
    served = terms[0][0].shape[1]
    tile = min(served, 256)
    places, first_column, width = placing or (0, 0, 0)
    where = [active, places, first_column, active | places]
    for _, segments in terms:
        for _, offset, row, _, _ in segments:
            where += [offset, row]
    layout = [[(used.index(j), start, depth) for j, _, _, start, depth in segments] for _, segments in terms]
    count = sum(len(segments) for segments in layout)
    added = () if total is None else (total,)
    held = () if rollout is None else (rollout,)
    column = lambda i, where: (0, i)
    read = lambda i, where: (0, i * where[3])
    anywhere = pl.BlockSpec(memory_space=pl.ANY)
    fresh_shape, fresh_spec = jax.ShapeDtypeStruct((rows, served), jnp.float32), pl.BlockSpec((rows, tile), column)
    return pl.pallas_call(
        functools.partial(project_kernel, layout, len(lhs), bool(added), bool(held), placing is not None),
        out_shape=[fresh_shape, jax.ShapeDtypeStruct((D, width), jnp.bfloat16)] if placing else fresh_shape,
        grid_spec=pltpu.PrefetchScalarGridSpec(
            num_scalar_prefetch=1,
            grid=(served // tile,),
            in_specs=[pl.BlockSpec(part.shape, lambda i, where: (0, 0)) for part in lhs]
            + [pl.BlockSpec((block.shape[0], tile), read) for block, _ in terms]
            + [fresh_spec for _ in added]
            + [anywhere for _ in held],
            out_specs=[fresh_spec, anywhere] if placing else fresh_spec,
            scratch_shapes=[pltpu.SemaphoreType.DMA((count,))] if placing else [],
        ),
        input_output_aliases={1 + len(lhs) + len(terms) + len(added): 1} if held else {},
        compiler_params=pltpu.CompilerParams(vmem_limit_bytes=VMEM),
        cost_estimate=SHORT,
    )(jnp.stack([jnp.asarray(v, jnp.int32) for v in where]), *lhs, *[block for block, _ in terms], *added, *held)


def attend_kernel(share, active_ref, bias_ref, x_ref, q_ref, c_ref, f_ref, held_ref, o_ref):
    heads = share * HALF
    scale = HD ** (-0.5)

    @pl.when(active_ref[0] == 0)
    def _():
        o_ref[...] = held_ref[...]

    @pl.when(active_ref[0] == 1)
    def _():
        bias = jnp.concatenate([bias_ref[0]] * heads, axis=0)
        for g in range(q_ref.shape[1] // (heads * HD)):
            lanes = [slice((g * heads + i) * HD, (g * heads + i + 1) * HD) for i in range(heads)]
            query = jnp.concatenate([q_ref[:, lane] for lane in lanes], axis=0)
            at = g * share * PAIR
            keys = c_ref[:, :, at : at + HD].reshape(ROW_TILE * LMAX, HD)
            values = c_ref[:, :, at + HD : at + PAIR].reshape(ROW_TILE * LMAX, HD)
            fresh = f_ref[:, g * PAIR : (g + 1) * PAIR].astype(jnp.bfloat16).astype(jnp.float32)
            new_key = jnp.concatenate([fresh[:, :HD]] * heads, axis=0)
            new_value = jnp.concatenate([fresh[:, HD:]] * heads, axis=0)
            old = lax.dot_general(query, keys, (((1,), (1,)), ((), ())), preferred_element_type=jnp.float32)
            old = old * scale + bias
            new = jnp.sum(query.astype(jnp.float32) * new_key, axis=1, keepdims=True) * scale
            highest = jnp.maximum(jnp.max(old, axis=1, keepdims=True), new)
            old = jnp.exp(old - highest)
            new = jnp.exp(new - highest)
            inverse = 1.0 / (jnp.sum(old, axis=1, keepdims=True) + new)
            old = (old * inverse).astype(jnp.bfloat16)
            new = (new * inverse).astype(jnp.bfloat16).astype(jnp.float32)
            mixed = jnp.dot(old, values, preferred_element_type=jnp.float32) + new * new_value
            for i, lane in enumerate(lanes):
                total = x_ref[:, lane].astype(jnp.float32) + mixed[i * ROW_TILE : (i + 1) * ROW_TILE, :]
                o_ref[:, lane] = total.astype(jnp.bfloat16)


def seen_bias(lengths):
    column = jnp.arange(ROW_TILE * LMAX)
    own = jnp.arange(ROW_TILE)[:, None] == column[None, :] // LMAX
    seen = own[None] & ((column % LMAX)[None, None, :] < lengths.reshape(-1, ROW_TILE, 1))
    return jnp.where(seen, 0.0, -jnp.inf).astype(jnp.float32)


def attend(active, current, query, cache, bias, fresh, held):
    rows, width = query.shape
    share = min(2, width // (HALF * HD))
    wide = pl.BlockSpec((ROW_TILE, width), lambda i, active: (i, 0))
    return pl.pallas_call(
        functools.partial(attend_kernel, share),
        out_shape=jax.ShapeDtypeStruct((rows, width), jnp.bfloat16),
        grid_spec=pltpu.PrefetchScalarGridSpec(
            num_scalar_prefetch=1,
            grid=(rows // ROW_TILE,),
            in_specs=[
                pl.BlockSpec((1, *bias.shape[1:]), lambda i, active: (i, 0, 0)),
                wide,
                wide,
                pl.BlockSpec((ROW_TILE, LMAX, cache.shape[2]), lambda i, active: (i, 0, 0)),
                pl.BlockSpec((ROW_TILE, fresh.shape[1]), lambda i, active: (i, 0)),
                wide,
            ],
            out_specs=wide,
        ),
        compiler_params=pltpu.CompilerParams(vmem_limit_bytes=VMEM),
        cost_estimate=SHORT,
    )(active.reshape(1), bias, current, query, cache, fresh, held)


def together(*values):
    return lax.optimization_barrier(values)


def body(hidden_in, norm_gain, trainer_kv, queries, kv_cache, cache_lengths):
    sections, tensors, dps = (lax.axis_size(axis) for axis in ("section", "tensor", "dp"))
    section, tensor, dp = (lax.axis_index(axis) for axis in ("section", "tensor", "dp"))
    rows = hidden_in.shape[1]
    depth = trainer_kv.shape[1]
    own_width = 2 * KVH * HD // tensors
    served = max(own_width, PAIR)
    early, late = (1, 2), (0, 3)
    everyone = tuple(range(sections))
    is_early = ((section == 1) | (section == 2)).astype(jnp.int32)
    inner = (dp == 1) | (dp == 2)

    def over(axis, count, value, routes):
        pairs = [(a * count + i, b * count + j) for a, b, i, j in routes]
        return lax.ppermute(value, ("section", axis), pairs)

    def over_dp(value, at, target):
        return over("dp", dps, value, [(s, s, z, target[z]) for s in at for z in range(dps)])

    def over_tensor(value, at, flip, step=0):
        return over("tensor", tensors, value, [(s, s + step, t, t ^ flip) for s in at for t in range(tensors)])

    def flipped(b):
        return [z ^ b for z in range(dps)]

    def feature_block(value, b):
        return lax.dynamic_slice_in_dim(value, (dp ^ b) * depth, depth, 1)

    def normed_of(parts, inverse, gains):
        return [
            (part.astype(jnp.float32) * inverse[:, None] * gain.astype(jnp.float32)).astype(jnp.bfloat16)
            for part, gain in zip(parts, gains)
        ]

    def square_sum(part):
        wide = part.astype(jnp.float32)
        return jnp.sum(wide * wide, axis=1)

    bias = seen_bias(cache_lengths[0])
    turn = [(section == tick).astype(jnp.int32) for tick in range(sections)]

    def attended(tick, current, fresh, held):
        return attend(turn[tick], current, queries[0, 0], kv_cache[0, 0], bias, fresh, held)

    def hop(value, tick):
        return [over_tensor(value, (tick - 1,), j, 1) for j in range(tensors)]

    def prepared(parts):
        inverse = lax.rsqrt(sum(square_sum(part) for part in parts) / D + epsilon)
        return normed_of(parts, inverse, gains)

    halves = [[(0, 0)], [(j, (j - 1) * depth) for j in range(1, tensors)]]

    def relay(blocks):
        return jnp.where(inner, blocks[3], blocks[0])

    relay_to = (2, 0, 3, 1)

    def terms_of(half, blocks, which, shift=0):
        return [
            (
                blocks[b],
                [
                    (j, (dp ^ b) * depth + shift, ((tensor ^ j) * dps + (dp ^ b)) * depth, start, depth)
                    for j, start in halves[half]
                ],
            )
            for b in which
        ]

    def placing(active):
        return (active, tensor * own_width % served, own_width)

    kept = requantize(trainer_kv[0], [(tensor ^ j) * own_width // served * served for j in range(tensors)], served)
    hidden, kept = together(hidden_in[0], kept)

    squares = square_sum(hidden)
    for j in (2**i for i in range(tensors.bit_length() - 1)):
        squares = squares + over_tensor(squares, (0,), j)
    (normed,) = normed_of([hidden], lax.rsqrt(squares / D + epsilon), [norm_gain])
    first = [feature_block(normed, b) for b in range(dps)]
    first[1:] = [over_dp(first[b], (0,), flipped(b)) for b in range(1, dps)]
    gains = [norm_gain] + [over_tensor(norm_gain, everyone, j) for j in range(1, tensors)]

    def others(at, kept):
        received = [over_tensor(kept[j], at, j) for j in range(1, tensors)]
        return received[0] if len(received) == 1 else jnp.concatenate(received, axis=0)

    own = {0: kept[0], 3: over_dp(kept[0], early, flipped(3)), 1: over_dp(kept[0], early, flipped(1))}

    lhs = [jnp.concatenate(first, axis=0)]
    partial = [project(turn[0], lhs, [(kept[j], [(0, 0, 0, 0, depth)])]) for j in range(tensors)]
    partial, kept = together(partial, kept)
    rest = {0: others(early, kept)}
    total = partial[0]
    for j in range(1, tensors):
        total = total + over_tensor(partial[j], (0,), j)
    total = total.reshape(dps, rows, served)
    returned = [over_dp(total[b].astype(jnp.bfloat16), (0,), flipped(b)) for b in range(1, dps)]
    fresh = total[0]
    for part in returned:
        fresh = fresh + part.astype(jnp.float32)
    result = attended(0, hidden, fresh, hidden)

    rest[3], rest[1] = over_dp(rest[0], early, flipped(3)), over_dp(rest[0], early, flipped(1))
    own, result, kept = together(own, result, kept)
    own[2] = over_dp(relay(own), early, relay_to)
    own[2], rest = together(own[2], rest)
    handed = relay(rest)
    rest[2] = over_dp(handed, early, relay_to)
    token = over("dp", dps, handed[:ROW_TILE, :HD], [(a, b, z, z) for a, b in ((1, 0), (2, 3)) for z in range(dps)])
    token, late_block, result, kept = together(token, kept[0], result, kept)
    shift = jnp.isnan(token[0, 0]).astype(jnp.int32)
    late_own = {0: late_block, 3: over_dp(late_block, late, flipped(3)), 1: over_dp(late_block, late, flipped(1))}
    moved = hop(result, 1)
    late_rest = {0: others(late, kept)}

    terms = terms_of(0, own, range(dps)) + terms_of(1, rest, range(dps))
    fresh, rollout = project(turn[1], prepared(moved), terms, None, placing(is_early))
    result = attended(1, moved[0], fresh, result)

    late_rest[0], result = together(late_rest[0], result)
    late_rest[3], late_rest[1] = over_dp(late_rest[0], late, flipped(3)), over_dp(late_rest[0], late, flipped(1))
    moved = hop(result, 2)
    late_own, moved = together(late_own, moved)
    late_own[2] = over_dp(relay(late_own), late, relay_to)
    result = attended(2, moved[0], project(turn[2], prepared(moved), terms), result)
    moved = hop(result, 3)

    normed = prepared(moved)
    late_own, late_rest, normed = together(late_own, late_rest, normed)
    late_rest[2] = over_dp(relay(late_rest), late, relay_to)
    terms = terms_of(0, late_own, range(dps), shift) + terms_of(1, late_rest, (0, 1, 3))
    fresh, rollout = project(turn[3], normed, terms, None, placing(1 - is_early), rollout)
    fresh, rollout, late_rest[2] = together(fresh, rollout, late_rest[2])
    fresh, rollout = project(turn[3], normed, terms_of(1, late_rest, (2,)), fresh, placing(1 - is_early), rollout)
    result = attended(3, moved[0], fresh, result)
    return (rollout[None], result[None, None])


def solution(mesh):
    placed = (
        P(None, "dp", "tensor"),
        P("section", "tensor"),
        P("section", ("tensor", "dp"), None),
        P("section", None, "dp", "tensor"),
        P("section", None, "dp", None, "tensor"),
        P(None, "dp"),
    )
    return jax.shard_map(
        body,
        mesh=mesh,
        in_specs=placed,
        out_specs=(P("section", None, "tensor"), P("section", None, "dp", "tensor")),
        check_vma=False,
    )
```

time: 665 us -> 673 us (1.012)
  waiting for transfers between devices: 321 us -> 381 us
  Pallas kernels: 141 us -> 109 us
  local copies, waits for them, and re-layouts: 25.9 us -> 6.8 us
    ppermute x30, waiting for transfers between devices: 321 us -> 381 us  [over(): return lax.ppermute(value, ('section', axis), pairs)]
    pallas_call x6, Pallas kernels: 80 us -> 60.2 us  [project(): pl.pallas_call(functools.partial(project_kernel, layout, len(lhs), bool(a...]
    pallas_call x4, Pallas kernels: 50.6 us -> 38 us  [attend(): pl.pallas_call(functools.partial(attend_kernel, share), out_shape=jax.Sha...]
    reshape x1 -> x0, local copies, waits for them, and re-layouts: 12.5 us -> none  [seen_bias(): return bias.reshape(-1, heads * ROW_TILE, ROW_TILE * LMAX)]
    broadcast_in_dim x1 -> x0, local copies, waits for them, and re-layouts: 8.26 us -> none  [seen_bias(): jnp.broadcast_to(bias[:, None], (bias.shape[0], heads, ROW_TILE, ROW_TILE...]
    select_n x6 -> x7, other arithmetic: 18.1 us -> 16.9 us  [the longest x4 16.1 us: relay(): return jnp.where(inner, blocks[3], blocks[0])]
  transfers between devices with their start and end apart: 30 -> 30, of which waited for: 13 -> 14; matrix products, arithmetic and copies ran while one was open for 10% -> 6% of each run, Pallas kernels for 16% -> 12%
where the time goes in v1:
time: 673 us; the launch traced here: 671 us
  waiting for transfers between devices  381 us (57%)
  starting transfers between devices  126 us (19%)
  Pallas kernels  109 us (16%)
  other arithmetic  46.1 us (7%)
  local copies, waits for them, and re-layouts  6.8 us (1%)
    ppermute x30, waiting for transfers between devices, over(): return lax.ppermute(value, ('section', axis), pairs)  381 us
    ppermute x30, starting transfers between devices, over(): return lax.ppermute(value, ('section', axis), pairs)  126 us
    pallas_call x6, Pallas kernels, project(): pl.pallas_call(functools.partial(project_kernel, layout, len(lhs), bool(a...  60.2 us
    pallas_call x4, Pallas kernels, attend(): pl.pallas_call(functools.partial(attend_kernel, share), out_shape=jax.Sha...  38 us
    select_n x4, other arithmetic, relay(): return jnp.where(inner, blocks[3], blocks[0])  16.1 us
    convert_element_type x4, other arithmetic, normed_of(): (part.astype(jnp.float32) * inverse[:, None] * gain.astype(jnp.float32))....  13.5 us
  transfers between devices with their start and end apart: 30, of which 14 were waited for; matrix products, arithmetic and copies ran while one was open for 6% of the time, Pallas kernels for 12%

profile of v1, /device:TPU:0, one launch (start us, length us, event | category | flops | bytes accessed | tf_op | source)
XLA Modules:
  0.0 670.8 jit_solution(5847642127467861982)
XLA Ops:
  1.3 10.3 %shard_map.77 = (bf16[2048,1024]{1,0:T(8,128)(2,1)}, bf16[2048,1024]{1,0:T(8,128)(2,1)}) custom-call(s32[2]{0:T(128)} %pad_add_fusion.column_ref, bf16[2048,2048]{1,0:T(8,128)(2,1)} %bitcast.49), custom_call_target="tpu_custom_call" | custom-call | tf_op jit(solution)/shard_map/pallas_call | solution.py:42
  12.1 4.9 collective-permute-start.2
  17.0 1.4 collective-permute-done.2
  19.4 6.0 collective-permute-start.5
  25.4 1.9 collective-permute-start.4
  27.3 2.5 collective-permute-start.3
  29.8 2.6 collective-permute-start.1
  32.4 2.6 collective-permute-start
  35.7 2.6 collective-permute-done.5
  38.4 64.9 %collective-permute-done.4 = bf16[128,2048]{1,0:T(8,128)(2,1)S(1)} collective-permute-done((bf16[128,2048]{1,0:T(8,128)(2,1)S(1)}, bf16[128,2048]{1,0:T(8,128)(2,1)S(1)}, u32[]{:S(2)}, u32[]{:S(2)}) %collective-permute-start.4) | collective-permute-done | bytes 524320 | tf_op jit(solution)/shard_map/ppermute | solution.py:230
  103.3 2.5 pad_maximum_fusion.refs_0_
  105.8 7.1 %shard_map.78 = f32[512,1024]{1,0:T(8,128)} custom-call(s32[6]{0:T(128)} %pad_add_fusion.1.where_ref, bf16[512,2048]{1,0:T(8,128)(2,1)} %pad_maximum_fusion.refs_0_, bf16[2048,1024]{1,0:T(8,128)(2,1)} %get-tuple-element.83.refs_1_.refs_2_), custom_call_target="tpu_custom_call" | custom-call | tf_op jit(solution)/shard_map/pallas_call | solution.py:126
  112.9 7.3 %shard_map.79 = f32[512,1024]{1,0:T(8,128)} custom-call(s32[6]{0:T(128)} %pad_add_fusion.1.where_ref, bf16[512,2048]{1,0:T(8,128)(2,1)} %pad_maximum_fusion.refs_0_, bf16[2048,1024]{1,0:T(8,128)(2,1)} %get-tuple-element.67.refs_1_), custom_call_target="tpu_custom_call" | custom-call | tf_op jit(solution)/shard_map/pallas_call | solution.py:126
  120.2 3.5 collective-permute-start.6
  123.8 2.7 collective-permute-start.11
  126.5 22.0 %collective-permute-done.6 = f32[512,1024]{1,0:T(8,128)S(1)} collective-permute-done((f32[512,1024]{1,0:T(8,128)}, f32[512,1024]{1,0:T(8,128)S(1)}, u32[]{:S(2)}, u32[]{:S(2)}) %collective-permute-start.6) | collective-permute-done | bytes 2097184 | tf_op jit(solution)/shard_map/ppermute | solution.py:230
  148.5 1.8 fusion.25
  150.4 2.6 collective-permute-start.7
  153.0 4.7 collective-permute-start.9
  157.8 3.7 collective-permute-done.7
  161.5 4.0 collective-permute-start.8
  167.5 1.2 collective-permute-done.9
  168.7 83.5 %collective-permute-done.8 = bf16[128,1024]{1,0:T(8,128)(2,1)S(1)} collective-permute-done((bf16[128,1024]{1,0:T(8,128)(2,1)S(1)}, bf16[128,1024]{1,0:T(8,128)(2,1)S(1)}, u32[]{:S(2)}, u32[]{:S(2)}) %collective-permute-start.8) | collective-permute-done | bytes 262176 | tf_op jit(solution)/shard_map/ppermute | solution.py:230
  252.2 2.0 fusion.22.f_ref
  254.1 13.3 %shard_map.80.held_ref = bf16[128,8192]{1,0:T(8,128)(2,1)} custom-call(s32[1]{0:T(128)} %bitcast.10.active_ref, f32[8,16,256]{2,1,0:T(8,128)} %and_select_fusion.bias_ref, bf16[128,8192]{1,0:T(8,128)(2,1)} %bitcast.45, bf16[128,8192]{1,0:T(8,128)(2,1)} %bitcast.41, bf16[128,16,2048]{2,1,0:T(8,128)(2,1)} %bitcast.36, f32[128,1024]{1,0:T(8,128)} %fusion.22.f_ref, ...), custom_call_target="tpu_custom_call" | custom-call | tf_op jit(solution)/shard_map/pallas_call | solution.py:191
  267.4 2.6 broadcast_select_fusion.3
  270.1 0.9 collective-permute-start.10
  272.0 2.6 collective-permute-start.12
  274.6 2.0 copy-done.5
  276.6 6.3 broadcast_select_fusion.2
  283.5 1.3 collective-permute-start.14
  284.8 8.4 %collective-permute-done.14 = bf16[16,128]{1,0:T(8,128)(2,1)S(1)} collective-permute-done((bf16[16,128]{1,0:T(8,128)(2,1)S(1)}, bf16[16,128]{1,0:T(8,128)(2,1)S(1)}, u32[]{:S(2)}, u32[]{:S(2)}) %collective-permute-start.14) | collective-permute-done | bytes 4128 | tf_op jit(solution)/shard_map/ppermute | solution.py:230
  293.2 4.6 collective-permute-start.19
  297.8 1.4 collective-permute-start.18
  299.2 2.7 collective-permute-start.21
  301.9 2.4 collective-permute-start.17
  304.3 1.6 collective-permute-start.20
  306.6 60.2 %collective-permute-done.20 = bf16[1,8192]{1,0:T(2,128)(2,1)S(1)} collective-permute-done((bf16[1,8192]{1,0:T(2,128)(2,1)S(1)}, bf16[1,8192]{1,0:T(2,128)(2,1)S(1)}, u32[]{:S(2)}, u32[]{:S(2)}) %collective-permute-start.20) | collective-permute-done | bytes 16416 | tf_op jit(solution)/shard_map/ppermute | solution.py:230
  366.8 3.7 collective-permute-start.16
  370.6 5.1 collective-permute-start.15
  375.7 2.1 fusion.6
  378.3 4.9 fusion.8
  383.2 7.2 %shard_map.81 = (f32[128,1024]{1,0:T(8,128)}, bf16[16384,1024]{1,0:T(8,128)(2,1)}) custom-call(s32[20]{0:T(128)} %stack.158.where_ref, bf16[128,8192]{1,0:T(8,128)(2,1)} %get-tuple-element.112.refs_0_, bf16[128,8192]{1,0:T(8,128)(2,1)} %get-tuple-element.111.refs_1_, bf16[2048,1024]{1,0:T(8,128)(2,1)} %get-tuple-element.83.refs_1_.refs_2_, ...), custom_call_target="tpu_custom_call" | custom-call | tf_op jit(solution)/shard_map/pallas_call | solution.py:126
  390.5 8.2 %shard_map.82.held_ref = bf16[128,8192]{1,0:T(8,128)(2,1)} custom-call(s32[1]{0:T(128)} %bitcast.14.active_ref, f32[8,16,256]{2,1,0:T(8,128)} %and_select_fusion.bias_ref, bf16[128,8192]{1,0:T(8,128)(2,1)} %copy-done.3, bf16[128,8192]{1,0:T(8,128)(2,1)} %bitcast.42, bf16[128,16,2048]{2,1,0:T(8,128)(2,1)} %bitcast.37, f32[128,1024]{1,0:T(8,128)} %get-tuple-element.72.f_ref, ...), custom_call_target="tpu_custom_call" | custom-call | tf_op jit(solution)/shard_map/pallas_call | solution.py:191
  398.7 2.0 collective-permute-start.23
  402.2 3.2 collective-permute-start.26
  405.4 14.1 %collective-permute-done.16.refs_5_ = bf16[2048,1024]{1,0:T(8,128)(2,1)} collective-permute-done((bf16[2048,1024]{1,0:T(8,128)(2,1)}, bf16[2048,1024]{1,0:T(8,128)(2,1)}, u32[]{:S(2)}, u32[]{:S(2)}) %collective-permute-start.16) | collective-permute-done | bytes 4194336 | tf_op jit(solution)/shard_map/ppermute | solution.py:230
  419.5 47.2 %collective-permute-start.25 = (bf16[2048,1024]{1,0:T(8,128)(2,1)}, bf16[2048,1024]{1,0:T(8,128)(2,1)}, u32[]{:S(2)}, u32[]{:S(2)}) collective-permute-start(bf16[2048,1024]{1,0:T(8,128)(2,1)} %collective-permute-done.17.refs_6_), channel_id=1, source_target_pairs={{0,1},{1,0},{2,3},{3,2},{24,25},{25,24},{26,27},{27,26},{4,5},{5,4... | collective-permute-start | bytes 12582920 | tf_op jit(solution)/shard_map/ppermute | solution.py:230
  466.8 3.3 fusion.9
  470.0 4.7 fusion.14
  474.8 7.0 %shard_map.83.f_ref = f32[128,1024]{1,0:T(8,128)} custom-call(s32[20]{0:T(128)} %stack.159.where_ref, bf16[128,8192]{1,0:T(8,128)(2,1)} %get-tuple-element.110.refs_0_, bf16[128,8192]{1,0:T(8,128)(2,1)} %get-tuple-element.109.refs_1_, bf16[2048,1024]{1,0:T(8,128)(2,1)} %get-tuple-element.83.refs_1_.refs_2_, bf16[2048,1024]{1,0:T(8,128)(2,1)} %collective-permute-done.refs_3_, ...), custom_call_target="tpu_custom_call" | custom-call | tf_op jit(solution)/shard_map/pallas_call | solution.py:126
  481.8 8.2 %shard_map.84.held_ref = bf16[128,8192]{1,0:T(8,128)(2,1)} custom-call(s32[1]{0:T(128)} %bitcast.28.active_ref, f32[8,16,256]{2,1,0:T(8,128)} %and_select_fusion.bias_ref, bf16[128,8192]{1,0:T(8,128)(2,1)} %copy-done.2, bf16[128,8192]{1,0:T(8,128)(2,1)} %bitcast.43, bf16[128,16,2048]{2,1,0:T(8,128)(2,1)} %bitcast.38, f32[128,1024]{1,0:T(8,128)} %shard_map.83.f_ref, ...), custom_call_target="tpu_custom_call" | custom-call | tf_op jit(solution)/shard_map/pallas_call | solution.py:191
  491.6 2.6 broadcast_select_fusion.1
  494.2 2.5 collective-permute-start.24
  497.8 3.2 fusion.20
  501.0 8.5 %collective-permute-done.26.refs_8_ = bf16[2048,1024]{1,0:T(8,128)(2,1)} collective-permute-done((bf16[2048,1024]{1,0:T(8,128)(2,1)}, bf16[2048,1024]{1,0:T(8,128)(2,1)}, u32[]{:S(2)}, u32[]{:S(2)}) %collective-permute-start.26) | collective-permute-done | bytes 4194336 | tf_op jit(solution)/shard_map/ppermute | solution.py:230
  509.5 44.8 %collective-permute-done.25.refs_7_ = bf16[2048,1024]{1,0:T(8,128)(2,1)} collective-permute-done((bf16[2048,1024]{1,0:T(8,128)(2,1)}, bf16[2048,1024]{1,0:T(8,128)(2,1)}, u32[]{:S(2)}, u32[]{:S(2)}) %collective-permute-start.25) | collective-permute-done | bytes 4194336 | tf_op jit(solution)/shard_map/ppermute | solution.py:230
  554.3 44.9 %collective-permute-done.24.refs_4_ = bf16[2048,1024]{1,0:T(8,128)(2,1)} collective-permute-done((bf16[2048,1024]{1,0:T(8,128)(2,1)S(1)}, bf16[2048,1024]{1,0:T(8,128)(2,1)}, u32[]{:S(2)}, u32[]{:S(2)}) %collective-permute-start.24) | collective-permute-done | bytes 4194336 | tf_op jit(solution)/shard_map/ppermute | solution.py:230
  599.3 4.6 broadcast_select_fusion
  603.9 2.8 collective-permute-start.29
  609.8 23.6 %shard_map.85 = (f32[128,1024]{1,0:T(8,128)}, bf16[16384,1024]{1,0:T(8,128)(2,1)}) custom-call(s32[18]{0:T(128)} %stack.164.where_ref, bf16[128,8192]{1,0:T(8,128)(2,1)} %get-tuple-element.82.refs_0_, bf16[128,8192]{1,0:T(8,128)(2,1)} %get-tuple-element.80.refs_1_.refs_0_, ...), custom_call_target="tpu_custom_call", output_to_operand_aliasing={{1}: (10, {})} | custom-call | tf_op jit(solution)/shard_map/pallas_call | solution.py:126
  633.4 21.1 %collective-permute-done.29.refs_1_ = bf16[2048,1024]{1,0:T(8,128)(2,1)} collective-permute-done((bf16[2048,1024]{1,0:T(8,128)(2,1)}, bf16[2048,1024]{1,0:T(8,128)(2,1)}, u32[]{:S(2)}, u32[]{:S(2)}) %collective-permute-start.29) | collective-permute-done | bytes 4194336 | tf_op jit(solution)/shard_map/ppermute | solution.py:230
  654.6 8.0 %shard_map.86 = (f32[128,1024]{1,0:T(8,128)}, bf16[16384,1024]{1,0:T(8,128)(2,1)}) custom-call(s32[6]{0:T(128)} %stack.66.where_ref, bf16[128,8192]{1,0:T(8,128)(2,1)} %get-tuple-element.80.refs_1_.refs_0_, bf16[2048,1024]{1,0:T(8,128)(2,1)} %collective-permute-done.29.refs_1_, ...), custom_call_target="tpu_custom_call", output_to_operand_aliasing={{1}: (4, {})} | custom-call | tf_op jit(solution)/shard_map/pallas_call | solution.py:126
  662.5 8.2 %shard_map.87 = bf16[128,8192]{1,0:T(8,128)(2,1)} custom-call(s32[1]{0:T(128)} %bitcast.active_ref, f32[8,16,256]{2,1,0:T(8,128)} %and_select_fusion.bias_ref, bf16[128,8192]{1,0:T(8,128)(2,1)} %copy-done.4, bf16[128,8192]{1,0:T(8,128)(2,1)} %bitcast.44, bf16[128,16,2048]{2,1,0:T(8,128)(2,1)} %bitcast.39, f32[128,1024]{1,0:T(8,128)} %get-tuple-element.97.f_ref, ...), custom_call_target="tpu_custom_call" | custom-call | tf_op jit(solution)/shard_map/pallas_call | solution.py:191
  (66 shorter events, 13.6 us)
Async XLA Ops:
  1.3 10.3 %copy-start.1 = (bf16[1,128,8192]{2,1,0:T(8,128)(2,1)S(1)}, bf16[1,128,8192]{2,1,0:T(8,128)(2,1)}, u32[]{:S(2)}) copy-start(bf16[1,128,8192]{2,1,0:T(8,128)(2,1)} %param.6) | copy-start | bytes 6291460
  1.3 15.7 %copy-start.7 = (bf16[1,8192]{1,0:T(2,128)(2,1)S(1)}, bf16[1,8192]{1,0:T(2,128)(2,1)}, u32[]{:S(2)}) copy-start(bf16[1,8192]{1,0:T(2,128)(2,1)} %param.7) | copy-start | bytes 49156
  12.1 6.4 collective-permute-start.2
  19.4 19.0 %collective-permute-start.5 = (bf16[128,2048]{1,0:T(8,128)(2,1)S(1)}, bf16[128,2048]{1,0:T(8,128)(2,1)S(1)}, u32[]{:S(2)}, u32[]{:S(2)}) collective-permute-start(bf16[128,2048]{1,0:T(8,128)(2,1)S(1)} %get-tuple-element.101), channel_id=1, source_target_pairs={{0,3},{1,2},{2,1},{3,0},{4,7},{5,6},{6,5},{7,4}} | collective-permute-start | bytes 1572872 | tf_op jit(solution)/shard_map/ppermute | solution.py:230
  25.4 77.9 %collective-permute-start.4 = (bf16[128,2048]{1,0:T(8,128)(2,1)S(1)}, bf16[128,2048]{1,0:T(8,128)(2,1)S(1)}, u32[]{:S(2)}, u32[]{:S(2)}) collective-permute-start(bf16[128,2048]{1,0:T(8,128)(2,1)S(1)} %get-tuple-element.102), channel_id=1, source_target_pairs={{0,2},{1,3},{2,0},{3,1},{4,6},{5,7},{6,4},{7,5}} | collective-permute-start | bytes 1572872 | tf_op jit(solution)/shard_map/ppermute | solution.py:230
  27.3 76.0 %collective-permute-start.3 = (bf16[128,2048]{1,0:T(8,128)(2,1)S(1)}, bf16[128,2048]{1,0:T(8,128)(2,1)}, u32[]{:S(2)}, u32[]{:S(2)}) collective-permute-start(bf16[128,2048]{1,0:T(8,128)(2,1)S(1)} %get-tuple-element.103), channel_id=1, source_target_pairs={{0,1},{1,0},{2,3},{3,2},{4,5},{5,4},{6,7},{7,6}} | collective-permute-start | bytes 1572872 | tf_op jit(solution)/shard_map/ppermute | solution.py:230
  29.8 237.7 %collective-permute-start.1 = (bf16[2048,1024]{1,0:T(8,128)(2,1)}, bf16[2048,1024]{1,0:T(8,128)(2,1)}, u32[]{:S(2)}, u32[]{:S(2)}) collective-permute-start(bf16[2048,1024]{1,0:T(8,128)(2,1)} %get-tuple-element.83.refs_1_.refs_2_), channel_id=1, source_target_pairs={{8,11},{9,10},{10,9},{11,8},{16,19},{17,18},{18,17},{19,16},{12,15... | collective-permute-start | bytes 12582920 | tf_op jit(solution)/shard_map/ppermute | solution.py:230
  32.4 235.0 %collective-permute-start = (bf16[2048,1024]{1,0:T(8,128)(2,1)}, bf16[2048,1024]{1,0:T(8,128)(2,1)}, u32[]{:S(2)}, u32[]{:S(2)}) collective-permute-start(bf16[2048,1024]{1,0:T(8,128)(2,1)} %get-tuple-element.83.refs_1_.refs_2_), channel_id=1, source_target_pairs={{8,9},{9,8},{10,11},{11,10},{16,17},{17,16},{18,19},{19,18},{12,13... | collective-permute-start | bytes 12582920 | tf_op jit(solution)/shard_map/ppermute | solution.py:230
  112.9 35.5 %copy-start.6 = (f32[512,1024]{1,0:T(8,128)S(1)}, f32[512,1024]{1,0:T(8,128)}, u32[]{:S(2)}) copy-start(f32[512,1024]{1,0:T(8,128)} %shard_map.78) | copy-start | bytes 6291460
  120.2 45.8 %copy-start.8 = (s32[1,128]{1,0:T(1,128)S(1)}, s32[1,128]{1,0:T(1,128)}, u32[]{:S(2)}) copy-start(s32[1,128]{1,0:T(1,128)} %param.11) | copy-start | bytes 1540
  120.2 28.3 %collective-permute-start.6 = (f32[512,1024]{1,0:T(8,128)}, f32[512,1024]{1,0:T(8,128)S(1)}, u32[]{:S(2)}, u32[]{:S(2)}) collective-permute-start(f32[512,1024]{1,0:T(8,128)} %shard_map.79), channel_id=1, source_target_pairs={{0,4},{4,0},{1,5},{5,1},{2,6},{6,2},{3,7},{7,3}} | collective-permute-start | bytes 6291464 | tf_op jit(solution)/shard_map/ppermute | solution.py:230
  123.8 147.3 %collective-permute-start.11 = (bf16[2048,1024]{1,0:T(8,128)(2,1)}, bf16[2048,1024]{1,0:T(8,128)(2,1)}, u32[]{:S(2)}, u32[]{:S(2)}) collective-permute-start(bf16[2048,1024]{1,0:T(8,128)(2,1)} %get-tuple-element.67.refs_1_), channel_id=1, source_target_pairs={{8,12},{12,8},{16,20},{20,16},{9,13},{13,9},{17,21},{21,17},{10,14... | collective-permute-start | bytes 12582920 | tf_op jit(solution)/shard_map/ppermute | solution.py:230
  150.4 11.1 %collective-permute-start.7 = (bf16[128,1024]{1,0:T(8,128)(2,1)S(1)}, bf16[128,1024]{1,0:T(8,128)(2,1)S(1)}, u32[]{:S(2)}, u32[]{:S(2)}) collective-permute-start(bf16[128,1024]{1,0:T(8,128)(2,1)S(1)} %get-tuple-element.104), channel_id=1, source_target_pairs={{0,1},{1,0},{2,3},{3,2},{4,5},{5,4},{6,7},{7,6}} | collective-permute-start | bytes 786440 | tf_op jit(solution)/shard_map/ppermute | solution.py:230
  153.0 15.7 %collective-permute-start.9 = (bf16[128,1024]{1,0:T(8,128)(2,1)S(1)}, bf16[128,1024]{1,0:T(8,128)(2,1)S(1)}, u32[]{:S(2)}, u32[]{:S(2)}) collective-permute-start(bf16[128,1024]{1,0:T(8,128)(2,1)S(1)} %get-tuple-element.105), channel_id=1, source_target_pairs={{0,3},{1,2},{2,1},{3,0},{4,7},{5,6},{6,5},{7,4}} | collective-permute-start | bytes 786440 | tf_op jit(solution)/shard_map/ppermute | solution.py:230
  161.5 90.7 %collective-permute-start.8 = (bf16[128,1024]{1,0:T(8,128)(2,1)S(1)}, bf16[128,1024]{1,0:T(8,128)(2,1)S(1)}, u32[]{:S(2)}, u32[]{:S(2)}) collective-permute-start(bf16[128,1024]{1,0:T(8,128)(2,1)S(1)} %get-tuple-element.106), channel_id=1, source_target_pairs={{0,2},{1,3},{2,0},{3,1},{4,6},{5,7},{6,4},{7,5}} | collective-permute-start | bytes 786440 | tf_op jit(solution)/shard_map/ppermute | solution.py:230
  270.1 4.5 collective-permute-start.10
  271.0 3.5 collective-permute-start.13
  272.0 4.6 collective-permute-start.12
  274.6 2.0 copy-start.5
  276.6 6.3 copy-start
  283.5 9.7 %collective-permute-start.14 = (bf16[16,128]{1,0:T(8,128)(2,1)S(1)}, bf16[16,128]{1,0:T(8,128)(2,1)S(1)}, u32[]{:S(2)}, u32[]{:S(2)}) collective-permute-start(bf16[16,128]{1,0:T(8,128)(2,1)S(1)} %slice.35), channel_id=1, source_target_pairs={{8,0},{9,1},{10,2},{11,3},{16,24},{17,25},{18,26},{19,27},{12,4},{... | collective-permute-start | bytes 12296 | tf_op jit(solution)/shard_map/ppermute | solution.py:230
  293.2 77.3 %collective-permute-start.19 = (bf16[128,8192]{1,0:T(8,128)(2,1)}, bf16[128,8192]{1,0:T(8,128)(2,1)}, u32[]{:S(2)}, u32[]{:S(2)}) collective-permute-start(bf16[128,8192]{1,0:T(8,128)(2,1)} %shard_map.80.held_ref), channel_id=1, source_target_pairs={{0,12},{4,8},{1,13},{5,9},{2,14},{6,10},{3,15},{7,11}} | collective-permute-start | bytes 6291464 | tf_op jit(solution)/shard_map/ppermute | solution.py:230
  297.8 80.0 %collective-permute-start.18 = (bf16[128,8192]{1,0:T(8,128)(2,1)}, bf16[128,8192]{1,0:T(8,128)(2,1)S(1)}, u32[]{:S(2)}, u32[]{:S(2)}) collective-permute-start(bf16[128,8192]{1,0:T(8,128)(2,1)} %shard_map.80.held_ref), channel_id=1, source_target_pairs={{0,8},{4,12},{1,9},{5,13},{2,10},{6,14},{3,11},{7,15}} | collective-permute-start | bytes 6291464 | tf_op jit(solution)/shard_map/ppermute | solution.py:230
  299.2 84.0 %collective-permute-start.21 = (bf16[2048,1024]{1,0:T(8,128)(2,1)}, bf16[2048,1024]{1,0:T(8,128)(2,1)}, u32[]{:S(2)}, u32[]{:S(2)}) collective-permute-start(bf16[2048,1024]{1,0:T(8,128)(2,1)} %broadcast_select_fusion.2), channel_id=1, source_target_pairs={{8,10},{9,8},{10,11},{11,9},{16,18},{17,16},{18,19},{19,17},{12,14... | collective-permute-start | bytes 12582920 | tf_op jit(solution)/shard_map/ppermute | solution.py:230
  301.9 96.8 %collective-permute-start.17 = (bf16[2048,1024]{1,0:T(8,128)(2,1)}, bf16[2048,1024]{1,0:T(8,128)(2,1)}, u32[]{:S(2)}, u32[]{:S(2)}) collective-permute-start(bf16[2048,1024]{1,0:T(8,128)(2,1)} %get-tuple-element.67.refs_1_), channel_id=1, source_target_pairs={{0,4},{4,0},{24,28},{28,24},{1,5},{5,1},{25,29},{29,25},{2,6},{6,2... | collective-permute-start | bytes 12582920 | tf_op jit(solution)/shard_map/ppermute | solution.py:230
  304.3 62.4 %collective-permute-start.20 = (bf16[1,8192]{1,0:T(2,128)(2,1)S(1)}, bf16[1,8192]{1,0:T(2,128)(2,1)S(1)}, u32[]{:S(2)}, u32[]{:S(2)}) collective-permute-start(bf16[1,8192]{1,0:T(2,128)(2,1)S(1)} %copy-done.7), channel_id=1, source_target_pairs={{0,4},{4,0},{8,12},{12,8},{16,20},{20,16},{24,28},{28,24},{1,5},{5... | collective-permute-start | bytes 49160 | tf_op jit(solution)/shard_map/ppermute | solution.py:230
  366.8 52.7 %collective-permute-start.16 = (bf16[2048,1024]{1,0:T(8,128)(2,1)}, bf16[2048,1024]{1,0:T(8,128)(2,1)}, u32[]{:S(2)}, u32[]{:S(2)}) collective-permute-start(bf16[2048,1024]{1,0:T(8,128)(2,1)} %get-tuple-element.83.refs_1_.refs_2_), channel_id=1, source_target_pairs={{0,3},{1,2},{2,1},{3,0},{24,27},{25,26},{26,25},{27,24},{4,7},{5,6... | collective-permute-start | bytes 12582920 | tf_op jit(solution)/shard_map/ppermute | solution.py:230
  370.6 96.2 %collective-permute-start.15 = (bf16[2048,1024]{1,0:T(8,128)(2,1)}, bf16[2048,1024]{1,0:T(8,128)(2,1)}, u32[]{:S(2)}, u32[]{:S(2)}) collective-permute-start(bf16[2048,1024]{1,0:T(8,128)(2,1)} %get-tuple-element.83.refs_1_.refs_2_), channel_id=1, source_target_pairs={{0,1},{1,0},{2,3},{3,2},{24,25},{25,24},{26,27},{27,26},{4,5},{5,4... | collective-permute-start | bytes 12582920 | tf_op jit(solution)/shard_map/ppermute | solution.py:230
  377.8 5.4 copy-start.3
  398.7 68.0 %collective-permute-start.23 = (bf16[128,8192]{1,0:T(8,128)(2,1)}, bf16[128,8192]{1,0:T(8,128)(2,1)}, u32[]{:S(2)}, u32[]{:S(2)}) collective-permute-start(bf16[128,8192]{1,0:T(8,128)(2,1)} %shard_map.82.held_ref), channel_id=1, source_target_pairs={{8,20},{12,16},{9,21},{13,17},{10,22},{14,18},{11,23},{15,19}} | collective-permute-start | bytes 6291464 | tf_op jit(solution)/shard_map/ppermute | solution.py:230
  400.7 66.1 %collective-permute-start.22 = (bf16[128,8192]{1,0:T(8,128)(2,1)}, bf16[128,8192]{1,0:T(8,128)(2,1)S(1)}, u32[]{:S(2)}, u32[]{:S(2)}) collective-permute-start(bf16[128,8192]{1,0:T(8,128)(2,1)} %shard_map.82.held_ref), channel_id=1, source_target_pairs={{8,16},{12,20},{9,17},{13,21},{10,18},{14,22},{11,19},{15,23}} | collective-permute-start | bytes 6291464 | tf_op jit(solution)/shard_map/ppermute | solution.py:230
  402.2 107.3 %collective-permute-start.26 = (bf16[2048,1024]{1,0:T(8,128)(2,1)}, bf16[2048,1024]{1,0:T(8,128)(2,1)}, u32[]{:S(2)}, u32[]{:S(2)}) collective-permute-start(bf16[2048,1024]{1,0:T(8,128)(2,1)} %collective-permute-done.17.refs_6_), channel_id=1, source_target_pairs={{0,3},{1,2},{2,1},{3,0},{24,27},{25,26},{26,25},{27,24},{4,7},{5,6... | collective-permute-start | bytes 12582920 | tf_op jit(solution)/shard_map/ppermute | solution.py:230
  419.5 134.8 %collective-permute-start.25 = (bf16[2048,1024]{1,0:T(8,128)(2,1)}, bf16[2048,1024]{1,0:T(8,128)(2,1)}, u32[]{:S(2)}, u32[]{:S(2)}) collective-permute-start(bf16[2048,1024]{1,0:T(8,128)(2,1)} %collective-permute-done.17.refs_6_), channel_id=1, source_target_pairs={{0,1},{1,0},{2,3},{3,2},{24,25},{25,24},{26,27},{27,26},{4,5},{5,4... | collective-permute-start | bytes 12582920 | tf_op jit(solution)/shard_map/ppermute | solution.py:230
  466.8 8.0 %copy-start.2 = (bf16[128,8192]{1,0:T(8,128)(2,1)}, bf16[128,8192]{1,0:T(8,128)(2,1)S(1)}, u32[]{:S(2)}) copy-start(bf16[128,8192]{1,0:T(8,128)(2,1)S(1)} %collective-permute-done.22.x_ref) | copy-start | bytes 6291460
  490.0 6.7 %collective-permute-start.28 = (bf16[128,8192]{1,0:T(8,128)(2,1)}, bf16[128,8192]{1,0:T(8,128)(2,1)S(1)}, u32[]{:S(2)}, u32[]{:S(2)}) collective-permute-start(bf16[128,8192]{1,0:T(8,128)(2,1)} %shard_map.84.held_ref), channel_id=1, source_target_pairs={{16,28},{20,24},{17,29},{21,25},{18,30},{22,26},{19,31},{23,27}} | collective-permute-start | bytes 6291464 | tf_op jit(solution)/shard_map/ppermute | solution.py:230
  490.8 6.5 collective-permute-start.27
  494.2 105.0 %collective-permute-start.24 = (bf16[2048,1024]{1,0:T(8,128)(2,1)S(1)}, bf16[2048,1024]{1,0:T(8,128)(2,1)}, u32[]{:S(2)}, u32[]{:S(2)}) collective-permute-start(bf16[2048,1024]{1,0:T(8,128)(2,1)S(1)} %broadcast_select_fusion.1), channel_id=1, source_target_pairs={{0,2},{1,0},{2,3},{3,1},{24,26},{25,24},{26,27},{27,25},{4,6},{5,4... | collective-permute-start | bytes 12582920 | tf_op jit(solution)/shard_map/ppermute | solution.py:230
  497.3 3.7 copy-start.4
  603.9 50.7 %collective-permute-start.29 = (bf16[2048,1024]{1,0:T(8,128)(2,1)}, bf16[2048,1024]{1,0:T(8,128)(2,1)}, u32[]{:S(2)}, u32[]{:S(2)}) collective-permute-start(bf16[2048,1024]{1,0:T(8,128)(2,1)} %broadcast_select_fusion), channel_id=1, source_target_pairs={{0,2},{1,0},{2,3},{3,1},{24,26},{25,24},{26,27},{27,25},{4,6},{5,4... | collective-permute-start | bytes 12582920 | tf_op jit(solution)/shard_map/ppermute | solution.py:230

commit v2 on v1

--- a/solution.py
+++ b/solution.py
@@ -19,6 +19,7 @@
 
 epsilon = 1e-05
 clip_ratio = 2.0
+FAR, RELAYED = 4, 5
 FIXED = 4
 VMEM = 60 << 20
 SHORT = pl.CostEstimate(flops=0, bytes_accessed=0, transcendentals=0)
@@ -61,76 +62,95 @@
     if has_held:
         rest.pop(0)
     o_ref = rest.pop(0)
-    segments = [(block, *segment) for block, of_block in zip(blocks, layout) for segment in of_block]
-
-    def copies():
+    segments = [(n, *segment) for n, (_, of_block) in enumerate(layout) for segment in of_block]
+
+    def copy(i):
+        n, _, start, depth = segments[i]
         out, sems = rest
         width = min(out.shape[1], o_ref.shape[1])
-        for i, (block, _, start, depth) in enumerate(segments):
-            rows = pl.ds(pl.multiple_of(where_ref[FIXED + 2 * i + 1], GROUP), depth)
-            columns = pl.ds(pl.multiple_of(pl.program_id(0) * width, HD), width)
-            source = block.at[pl.ds(start, depth)]
-            if width < block.shape[1]:
-                source = block.at[pl.ds(start, depth), pl.ds(pl.multiple_of(where_ref[2], HD), width)]
-            yield pltpu.make_async_copy(source, out.at[rows, columns], sems.at[i])
-
-    if placed:
-
-        @pl.when(where_ref[1] == 1)
-        def _():
-            for copy in copies():
-                copy.start()
-
-    @pl.when(where_ref[0] == 1)
-    def _():
-        total = total_ref[...] if has_total else None
-        for i, (block, j, start, depth) in enumerate(segments):
-            columns = pl.ds(pl.multiple_of(where_ref[FIXED + 2 * i], GROUP), depth)
-            term = jnp.dot(
-                lhs[j][:, columns], block[start : start + depth, :], preferred_element_type=jnp.float32
-            )
-            total = term if total is None else total + term
+        rows = pl.ds(pl.multiple_of(where_ref[FIXED + len(layout) + 2 * i + 1], GROUP), depth)
+        columns = pl.ds(pl.multiple_of(pl.program_id(0) * width, HD), width)
+        source = blocks[n].at[pl.ds(start, depth)]
+        if width < blocks[n].shape[1]:
+            source = blocks[n].at[pl.ds(start, depth), pl.ds(pl.multiple_of(where_ref[2], HD), width)]
+        return pltpu.make_async_copy(source, out.at[rows, columns], sems.at[i])
+
+    def add(which):
+        total = o_ref[...]
+        for i in which:
+            n, j, start, depth = segments[i]
+            columns = pl.ds(pl.multiple_of(where_ref[FIXED + len(layout) + 2 * i], GROUP), depth)
+            rows = blocks[n][start : start + depth, :]
+            total += jnp.dot(lhs[j][:, columns], rows, preferred_element_type=jnp.float32)
         o_ref[...] = total
 
-    @pl.when(where_ref[0] == 0)
-    def _():
-        o_ref[...] = jnp.zeros(o_ref.shape, jnp.float32)
-
-    if placed:
-
-        @pl.when(where_ref[1] == 1)
-        def _():
-            for copy in copies():
-                copy.wait()
+    def start(which):
+        for i in which:
+            copy(i).start()
+
+    def wait(which):
+        for i in which:
+            copy(i).wait()
+
+    groups = [(None, [i for i, segment in enumerate(segments) if not layout[segment[0]][0]])]
+    for n, (gated, _) in enumerate(layout):
+        if gated:
+            groups.append((n, [i for i, segment in enumerate(segments) if segment[0] == n]))
+
+    for n, which in groups:
+        has = 1 if n is None else where_ref[FIXED + n]
+
+        if placed and which:
+            pl.when(where_ref[1] * has == 1)(functools.partial(start, which))
+
+    o_ref[...] = total_ref[...] if has_total else jnp.zeros(o_ref.shape, jnp.float32)
+    for n, which in groups:
+        if which:
+            has = 1 if n is None else where_ref[FIXED + n]
+            pl.when(where_ref[0] * has == 1)(functools.partial(add, which))
+
+    for n, which in groups:
+        has = 1 if n is None else where_ref[FIXED + n]
+
+        if placed and which:
+            pl.when(where_ref[1] * has == 1)(functools.partial(wait, which))
 
 
 def project(active, lhs, terms, total=None, placing=None, rollout=None):
-    used = sorted({segment[0] for _, segments in terms for segment in segments})
+    used = sorted({segment[0] for _, _, segments in terms for segment in segments})
     lhs = [lhs[j] for j in used]
     rows = lhs[0].shape[0]
     served = terms[0][0].shape[1]
     tile = min(served, 256)
     places, first_column, width = placing or (0, 0, 0)
     where = [active, places, first_column, active | places]
-    for _, segments in terms:
+    where += [1 if has is None else has for _, has, _ in terms]
+    for _, _, segments in terms:
         for _, offset, row, _, _ in segments:
             where += [offset, row]
-    layout = [[(used.index(j), start, depth) for j, _, _, start, depth in segments] for _, segments in terms]
-    count = sum(len(segments) for segments in layout)
+    layout = [
+        (has is not None, [(used.index(j), start, depth) for j, _, _, start, depth in segments])
+        for _, has, segments in terms
+    ]
+    count = sum(len(segments) for _, segments in layout)
     added = () if total is None else (total,)
     held = () if rollout is None else (rollout,)
     column = lambda i, where: (0, i)
-    read = lambda i, where: (0, i * where[3])
+
+    def read(n):
+        return lambda i, where: (0, i * where[3] * where[FIXED + n])
+
     anywhere = pl.BlockSpec(memory_space=pl.ANY)
     fresh_shape, fresh_spec = jax.ShapeDtypeStruct((rows, served), jnp.float32), pl.BlockSpec((rows, tile), column)
+    placed = int(placing is not None)
     return pl.pallas_call(
-        functools.partial(project_kernel, layout, len(lhs), bool(added), bool(held), placing is not None),
+        functools.partial(project_kernel, layout, len(lhs), bool(added), bool(held), placed),
         out_shape=[fresh_shape, jax.ShapeDtypeStruct((D, width), jnp.bfloat16)] if placing else fresh_shape,
         grid_spec=pltpu.PrefetchScalarGridSpec(
             num_scalar_prefetch=1,
             grid=(served // tile,),
             in_specs=[pl.BlockSpec(part.shape, lambda i, where: (0, 0)) for part in lhs]
-            + [pl.BlockSpec((block.shape[0], tile), read) for block, _ in terms]
+            + [pl.BlockSpec((term[0].shape[0], tile), read(n)) for n, term in enumerate(terms)]
             + [fresh_spec for _ in added]
             + [anywhere for _ in held],
             out_specs=[fresh_spec, anywhere] if placing else fresh_spec,
@@ -139,14 +159,14 @@
         input_output_aliases={1 + len(lhs) + len(terms) + len(added): 1} if held else {},
         compiler_params=pltpu.CompilerParams(vmem_limit_bytes=VMEM),
         cost_estimate=SHORT,
-    )(jnp.stack([jnp.asarray(v, jnp.int32) for v in where]), *lhs, *[block for block, _ in terms], *added, *held)
+    )(jnp.stack([jnp.asarray(v, jnp.int32) for v in where]), *lhs, *[term[0] for term in terms], *added, *held)
 
 
 def attend_kernel(share, active_ref, bias_ref, x_ref, q_ref, c_ref, f_ref, held_ref, o_ref):
     heads = share * HALF
     scale = HD ** (-0.5)
 
-    @pl.when(active_ref[0] == 0)
+    @pl.when((active_ref[0] == 0) & (pl.program_id(0) == 0))
     def _():
         o_ref[...] = held_ref[...]
 
@@ -187,7 +207,7 @@
 def attend(active, current, query, cache, bias, fresh, held):
     rows, width = query.shape
     share = min(2, width // (HALF * HD))
-    wide = pl.BlockSpec((ROW_TILE, width), lambda i, active: (i, 0))
+    wide = pl.BlockSpec((ROW_TILE, width), lambda i, active: (i * active[0], 0))
     return pl.pallas_call(
         functools.partial(attend_kernel, share),
         out_shape=jax.ShapeDtypeStruct((rows, width), jnp.bfloat16),
@@ -195,15 +215,16 @@
             num_scalar_prefetch=1,
             grid=(rows // ROW_TILE,),
             in_specs=[
-                pl.BlockSpec((1, *bias.shape[1:]), lambda i, active: (i, 0, 0)),
+                pl.BlockSpec((1, *bias.shape[1:]), lambda i, active: (i * active[0], 0, 0)),
                 wide,
                 wide,
-                pl.BlockSpec((ROW_TILE, LMAX, cache.shape[2]), lambda i, active: (i, 0, 0)),
-                pl.BlockSpec((ROW_TILE, fresh.shape[1]), lambda i, active: (i, 0)),
-                wide,
+                pl.BlockSpec((ROW_TILE, LMAX, cache.shape[2]), lambda i, active: (i * active[0], 0, 0)),
+                pl.BlockSpec((ROW_TILE, fresh.shape[1]), lambda i, active: (i * active[0], 0)),
+                pl.BlockSpec((ROW_TILE, width), lambda i, active: (0, 0)),
             ],
             out_specs=wide,
         ),
+        input_output_aliases={6: 0},
         compiler_params=pltpu.CompilerParams(vmem_limit_bytes=VMEM),
         cost_estimate=SHORT,
     )(active.reshape(1), bias, current, query, cache, fresh, held)
@@ -223,7 +244,7 @@
     early, late = (1, 2), (0, 3)
     everyone = tuple(range(sections))
     is_early = ((section == 1) | (section == 2)).astype(jnp.int32)
-    inner = (dp == 1) | (dp == 2)
+    inner = ((dp == 1) | (dp == 2)).astype(jnp.int32)
 
     def over(axis, count, value, routes):
         pairs = [(a * count + i, b * count + j) for a, b, i, j in routes]
@@ -266,22 +287,27 @@
 
     halves = [[(0, 0)], [(j, (j - 1) * depth) for j in range(1, tensors)]]
 
-    def relay(blocks):
-        return jnp.where(inner, blocks[3], blocks[0])
-
-    relay_to = (2, 0, 3, 1)
+    def far(at, blocks):
+        return over("dp", dps, blocks[0], [(s, s, a, b) for s in at for a, b in ((0, 2), (3, 1))])
+
+    def relayed(at, blocks):
+        return over("dp", dps, blocks[3], [(s, s, a, b) for s in at for a, b in ((2, 3), (1, 0))])
+
+    def around(at, blocks):
+        return over_dp(jnp.where(inner == 1, blocks[3], blocks[0]), at, (2, 0, 3, 1))
 
     def terms_of(half, blocks, which, shift=0):
-        return [
-            (
-                blocks[b],
-                [
-                    (j, (dp ^ b) * depth + shift, ((tensor ^ j) * dps + (dp ^ b)) * depth, start, depth)
-                    for j, start in halves[half]
-                ],
-            )
-            for b in which
-        ]
+        terms = []
+        for name in which:
+            b, has = {FAR: (2, inner), RELAYED: (2, 1 - inner)}.get(name, (name, None))
+            source = dp ^ b
+            terms.append((blocks[name], has, [
+                (j, source * depth + shift, ((tensor ^ j) * dps + source) * depth, start, depth)
+                for j, start in halves[half]
+            ]))
+        return terms
+
+    everything = (0, 1, 3, FAR, RELAYED)
 
     def placing(active):
         return (active, tensor * own_width % served, own_width)
@@ -304,7 +330,7 @@
     own = {0: kept[0], 3: over_dp(kept[0], early, flipped(3)), 1: over_dp(kept[0], early, flipped(1))}
 
     lhs = [jnp.concatenate(first, axis=0)]
-    partial = [project(turn[0], lhs, [(kept[j], [(0, 0, 0, 0, depth)])]) for j in range(tensors)]
+    partial = [project(turn[0], lhs, [(kept[j], None, [(0, 0, 0, 0, depth)])]) for j in range(tensors)]
     partial, kept = together(partial, kept)
     rest = {0: others(early, kept)}
     total = partial[0]
@@ -318,37 +344,37 @@
     result = attended(0, hidden, fresh, hidden)
 
     rest[3], rest[1] = over_dp(rest[0], early, flipped(3)), over_dp(rest[0], early, flipped(1))
-    own, result, kept = together(own, result, kept)
-    own[2] = over_dp(relay(own), early, relay_to)
-    own[2], rest = together(own[2], rest)
-    handed = relay(rest)
-    rest[2] = over_dp(handed, early, relay_to)
-    token = over("dp", dps, handed[:ROW_TILE, :HD], [(a, b, z, z) for a, b in ((1, 0), (2, 3)) for z in range(dps)])
+    own, result, kept, gains = together(own, result, kept, gains)
+    own[RELAYED], own[FAR] = relayed(early, own), far(early, own)
+    own, rest = together(own, rest)
+    rest[RELAYED], rest[FAR] = relayed(early, rest), far(early, rest)
+    token = over("dp", dps, rest[3][:ROW_TILE, :HD], [(a, b, z, z) for a, b in ((1, 0), (2, 3)) for z in range(dps)])
     token, late_block, result, kept = together(token, kept[0], result, kept)
     shift = jnp.isnan(token[0, 0]).astype(jnp.int32)
     late_own = {0: late_block, 3: over_dp(late_block, late, flipped(3)), 1: over_dp(late_block, late, flipped(1))}
     moved = hop(result, 1)
+    moved, rest, kept = together(moved, rest, kept)
     late_rest = {0: others(late, kept)}
 
-    terms = terms_of(0, own, range(dps)) + terms_of(1, rest, range(dps))
+    terms = terms_of(0, own, everything) + terms_of(1, rest, everything)
     fresh, rollout = project(turn[1], prepared(moved), terms, None, placing(is_early))
     result = attended(1, moved[0], fresh, result)
 
-    late_rest[0], result = together(late_rest[0], result)
+    moved = hop(result, 2)
+    result = attended(2, moved[0], project(turn[2], prepared(moved), terms), result)
+    late_own, late_rest[0], result = together(late_own, late_rest[0], result)
     late_rest[3], late_rest[1] = over_dp(late_rest[0], late, flipped(3)), over_dp(late_rest[0], late, flipped(1))
-    moved = hop(result, 2)
-    late_own, moved = together(late_own, moved)
-    late_own[2] = over_dp(relay(late_own), late, relay_to)
-    result = attended(2, moved[0], project(turn[2], prepared(moved), terms), result)
+    late_own[2] = around(late, late_own)
     moved = hop(result, 3)
 
     normed = prepared(moved)
     late_own, late_rest, normed = together(late_own, late_rest, normed)
-    late_rest[2] = over_dp(relay(late_rest), late, relay_to)
+    late_rest[RELAYED], late_rest[FAR] = relayed(late, late_rest), far(late, late_rest)
     terms = terms_of(0, late_own, range(dps), shift) + terms_of(1, late_rest, (0, 1, 3))
     fresh, rollout = project(turn[3], normed, terms, None, placing(1 - is_early), rollout)
-    fresh, rollout, late_rest[2] = together(fresh, rollout, late_rest[2])
-    fresh, rollout = project(turn[3], normed, terms_of(1, late_rest, (2,)), fresh, placing(1 - is_early), rollout)
+    fresh, rollout, late_rest = together(fresh, rollout, late_rest)
+    terms = terms_of(1, late_rest, (FAR, RELAYED))
+    fresh, rollout = project(turn[3], normed, terms, fresh, placing(1 - is_early), rollout)
     result = attended(3, moved[0], fresh, result)
     return (rollout[None], result[None, None])
 

time: 673 us -> 660 us (0.981)
  waiting for transfers between devices: 381 us -> 424 us
  starting transfers between devices: 126 us -> 94.4 us
  Pallas kernels: 109 us -> 94.5 us
  other arithmetic: 46.1 us -> 33.9 us
    ppermute x30 -> x33, waiting for transfers between devices: 381 us -> 424 us  [over(): return lax.ppermute(value, ('section', axis), pairs)]
    ppermute x30 -> x33, starting transfers between devices: 126 us -> 94.4 us  [over(): return lax.ppermute(value, ('section', axis), pairs)]
    pallas_call x4, Pallas kernels: 38 us -> 21.6 us  [attend(): pl.pallas_call(functools.partial(attend_kernel, share), out_shape=jax.Sha...]
    select_n x4 -> x1, other arithmetic: 16.1 us -> 2.64 us  [around(): jnp.where(inner == 1, blocks[3], blocks[0])]
  transfers between devices with their start and end apart: 30 -> 33, of which waited for: 14 -> 15; matrix products, arithmetic and copies ran while one was open for 6% -> 5% of each run, Pallas kernels for 12% -> 9%
where the time goes in v2:
time: 660 us; the launch traced here: 659 us
  waiting for transfers between devices  424 us (64%)
  Pallas kernels  94.5 us (14%)
  starting transfers between devices  94.4 us (14%)
  other arithmetic  33.9 us (5%)
  local copies, waits for them, and re-layouts  9.59 us (1%)
    ppermute x33, waiting for transfers between devices, over(): return lax.ppermute(value, ('section', axis), pairs)  424 us
    ppermute x33, starting transfers between devices, over(): return lax.ppermute(value, ('section', axis), pairs)  94.4 us
    pallas_call x6, Pallas kernels, project(): pl.pallas_call(functools.partial(project_kernel, layout, len(lhs), bool(a...  62.6 us
    pallas_call x4, Pallas kernels, attend(): pl.pallas_call(functools.partial(attend_kernel, share), out_shape=jax.Sha...  21.6 us
    convert_element_type x4, other arithmetic, normed_of(): (part.astype(jnp.float32) * inverse[:, None] * gain.astype(jnp.float32))....  13.4 us
  transfers between devices with their start and end apart: 33, of which 15 were waited for; matrix products, arithmetic and copies ran while one was open for 5% of the time, Pallas kernels for 9%

profile of v2, /device:TPU:0, one launch (start us, length us, event | category | flops | bytes accessed | tf_op | source)
XLA Modules:
  0.0 658.7 jit_solution(13722834166947324378)
XLA Ops:
  1.3 10.3 %shard_map.77 = (bf16[2048,1024]{1,0:T(8,128)(2,1)}, bf16[2048,1024]{1,0:T(8,128)(2,1)}) custom-call(s32[2]{0:T(128)} %pad_add_fusion.column_ref, bf16[2048,2048]{1,0:T(8,128)(2,1)} %bitcast.53), custom_call_target="tpu_custom_call" | custom-call | tf_op jit(solution)/shard_map/pallas_call | solution.py:43
  12.2 4.9 collective-permute-start.2
  17.1 1.4 collective-permute-done.2
  20.4 6.0 collective-permute-start.5
  26.4 1.9 collective-permute-start.4
  28.3 2.5 collective-permute-start.3
  30.8 2.6 collective-permute-start.1
  33.4 2.7 collective-permute-start
  36.7 2.9 collective-permute-done.5
  39.6 66.3 %collective-permute-done.4 = bf16[128,2048]{1,0:T(8,128)(2,1)} collective-permute-done((bf16[128,2048]{1,0:T(8,128)(2,1)}, bf16[128,2048]{1,0:T(8,128)(2,1)}, u32[]{:S(2)}, u32[]{:S(2)}) %collective-permute-start.4) | collective-permute-done | bytes 524320 | tf_op jit(solution)/shard_map/ppermute | solution.py:251
  105.9 2.9 pad_maximum_fusion.refs_0_
  108.8 7.1 %shard_map.78 = f32[512,1024]{1,0:T(8,128)} custom-call(s32[7]{0:T(128)} %stack.76.where_ref, bf16[512,2048]{1,0:T(8,128)(2,1)} %pad_maximum_fusion.refs_0_, bf16[2048,1024]{1,0:T(8,128)(2,1)} %get-tuple-element.108.refs_1_.refs_2_), custom_call_target="tpu_custom_call" | custom-call | tf_op jit(solution)/shard_map/pallas_call | solution.py:146
  115.9 7.2 %shard_map.79 = f32[512,1024]{1,0:T(8,128)} custom-call(s32[7]{0:T(128)} %stack.76.where_ref, bf16[512,2048]{1,0:T(8,128)(2,1)} %pad_maximum_fusion.refs_0_, bf16[2048,1024]{1,0:T(8,128)(2,1)} %get-tuple-element.84.refs_1_), custom_call_target="tpu_custom_call" | custom-call | tf_op jit(solution)/shard_map/pallas_call | solution.py:146
  123.1 2.6 collective-permute-start.13
  125.7 3.4 collective-permute-start.6
  129.2 24.7 %collective-permute-done.6 = f32[512,1024]{1,0:T(8,128)S(1)} collective-permute-done((f32[512,1024]{1,0:T(8,128)}, f32[512,1024]{1,0:T(8,128)S(1)}, u32[]{:S(2)}, u32[]{:S(2)}) %collective-permute-start.6) | collective-permute-done | bytes 2097184 | tf_op jit(solution)/shard_map/ppermute | solution.py:251
  153.9 3.4 fusion.25
  157.4 2.0 collective-permute-start.7
  159.4 4.7 collective-permute-start.9
  164.1 4.4 collective-permute-done.7
  168.5 3.3 collective-permute-start.8
  175.2 1.5 collective-permute-start.10
  176.8 75.6 %collective-permute-done.8 = bf16[128,1024]{1,0:T(8,128)(2,1)S(1)} collective-permute-done((bf16[128,1024]{1,0:T(8,128)(2,1)S(1)}, bf16[128,1024]{1,0:T(8,128)(2,1)S(1)}, u32[]{:S(2)}, u32[]{:S(2)}) %collective-permute-start.8) | collective-permute-done | bytes 262176 | tf_op jit(solution)/shard_map/ppermute | solution.py:251
  252.3 2.0 fusion.22.f_ref
  254.4 12.8 %shard_map.80.held_ref = bf16[128,8192]{1,0:T(8,128)(2,1)} custom-call(s32[1]{0:T(128)} %bitcast.12.active_ref, f32[8,16,256]{2,1,0:T(8,128)} %and_select_fusion.bias_ref, bf16[128,8192]{1,0:T(8,128)(2,1)} %bitcast.49, bf16[128,8192]{1,0:T(8,128)(2,1)} %bitcast.45, bf16[128,16,2048]{2,1,0:T(8,128)(2,1)} %bitcast.39, ...), custom_call_target="tpu_custom_call", output_to_operand_aliasing={{}: (6, {})} | custom-call | tf_op jit(solution)/shard_map/pallas_call | solution.py:211
  267.2 2.7 collective-permute-start.11
  270.0 2.7 collective-permute-start.12
  272.6 2.6 collective-permute-start.15
  275.3 2.6 collective-permute-start.14
  277.9 2.7 collective-permute-start.21
  280.6 2.7 collective-permute-start.22
  285.2 14.2 %collective-permute-done.16 = bf16[16,128]{1,0:T(8,128)(2,1)S(1)} collective-permute-done((bf16[16,128]{1,0:T(8,128)(2,1)S(1)}, bf16[16,128]{1,0:T(8,128)(2,1)S(1)}, u32[]{:S(2)}, u32[]{:S(2)}) %collective-permute-start.16) | collective-permute-done | bytes 4128 | tf_op jit(solution)/shard_map/ppermute | solution.py:251
  299.4 4.6 collective-permute-start.20
  304.0 1.6 collective-permute-start.19
  306.4 20.1 %collective-permute-done.20 = bf16[128,8192]{1,0:T(8,128)(2,1)} collective-permute-done((bf16[128,8192]{1,0:T(8,128)(2,1)}, bf16[128,8192]{1,0:T(8,128)(2,1)}, u32[]{:S(2)}, u32[]{:S(2)}) %collective-permute-start.20) | collective-permute-done | bytes 2097184 | tf_op jit(solution)/shard_map/ppermute | solution.py:251
  326.4 3.3 fusion.3
  329.7 4.7 fusion.8
  334.4 8.1 %shard_map.81 = (f32[128,1024]{1,0:T(8,128)}, bf16[16384,1024]{1,0:T(8,128)(2,1)}) custom-call(s32[34]{0:T(128)} %stack.89.where_ref, bf16[128,8192]{1,0:T(8,128)(2,1)} %get-tuple-element.138.refs_0_, bf16[128,8192]{1,0:T(8,128)(2,1)} %get-tuple-element.137.refs_1_, bf16[2048,1024]{1,0:T(8,128)(2,1)} %get-tuple-element.108.refs_1_.refs_2_, ...), custom_call_target="tpu_custom_call" | custom-call | tf_op jit(solution)/shard_map/pallas_call | solution.py:146
  342.5 2.9 shard_map.82.held_ref
  345.5 2.0 collective-permute-start.25
  348.2 4.1 collective-permute-start.18
  352.3 5.4 collective-permute-start.17
  357.7 2.4 collective-permute-start.23
  360.8 2.1 fusion.12
  363.4 5.0 fusion.14
  368.4 7.9 %shard_map.83.f_ref = f32[128,1024]{1,0:T(8,128)} custom-call(s32[34]{0:T(128)} %stack.90.where_ref, bf16[128,8192]{1,0:T(8,128)(2,1)} %get-tuple-element.136.refs_0_, bf16[128,8192]{1,0:T(8,128)(2,1)} %get-tuple-element.135.refs_1_, bf16[2048,1024]{1,0:T(8,128)(2,1)} %get-tuple-element.108.refs_1_.refs_2_, bf16[2048,1024]{1,0:T(8,128)(2,1)} %collective-permute-done.refs_3_, ...), custom_call_target="tpu_custom_call" | custom-call | tf_op jit(solution)/shard_map/pallas_call | solution.py:146
  376.3 2.9 shard_map.84.held_ref
  379.2 21.8 %collective-permute-done.18.refs_5_ = bf16[2048,1024]{1,0:T(8,128)(2,1)} collective-permute-done((bf16[2048,1024]{1,0:T(8,128)(2,1)}, bf16[2048,1024]{1,0:T(8,128)(2,1)}, u32[]{:S(2)}, u32[]{:S(2)}) %collective-permute-start.18) | collective-permute-done | bytes 4194336 | tf_op jit(solution)/shard_map/ppermute | solution.py:251
  400.9 44.8 %collective-permute-done.17.refs_3_ = bf16[2048,1024]{1,0:T(8,128)(2,1)} collective-permute-done((bf16[2048,1024]{1,0:T(8,128)(2,1)}, bf16[2048,1024]{1,0:T(8,128)(2,1)}, u32[]{:S(2)}, u32[]{:S(2)}) %collective-permute-start.17) | collective-permute-done | bytes 4194336 | tf_op jit(solution)/shard_map/ppermute | solution.py:251
  447.4 2.6 broadcast_select_fusion
  450.0 3.3 collective-permute-start.26
  453.3 3.6 collective-permute-start.28
  456.9 2.4 collective-permute-start.27
  460.3 3.1 fusion.20
  463.4 37.0 %collective-permute-done.26.refs_4_ = bf16[2048,1024]{1,0:T(8,128)(2,1)S(1)} collective-permute-done((bf16[2048,1024]{1,0:T(8,128)(2,1)S(1)}, bf16[2048,1024]{1,0:T(8,128)(2,1)S(1)}, u32[]{:S(2)}, u32[]{:S(2)}) %collective-permute-start.26) | collective-permute-done | bytes 4194336 | tf_op jit(solution)/shard_map/ppermute | solution.py:251
  500.4 2.1 copy-done.4
  502.5 44.0 %collective-permute-done.28.refs_8_ = bf16[2048,1024]{1,0:T(8,128)(2,1)} collective-permute-done((bf16[2048,1024]{1,0:T(8,128)(2,1)}, bf16[2048,1024]{1,0:T(8,128)(2,1)}, u32[]{:S(2)}, u32[]{:S(2)}) %collective-permute-start.28) | collective-permute-done | bytes 4194336 | tf_op jit(solution)/shard_map/ppermute | solution.py:251
  546.5 43.9 %collective-permute-done.27.refs_7_ = bf16[2048,1024]{1,0:T(8,128)(2,1)} collective-permute-done((bf16[2048,1024]{1,0:T(8,128)(2,1)}, bf16[2048,1024]{1,0:T(8,128)(2,1)}, u32[]{:S(2)}, u32[]{:S(2)}) %collective-permute-start.27) | collective-permute-done | bytes 4194336 | tf_op jit(solution)/shard_map/ppermute | solution.py:251
  590.4 6.0 collective-permute-start.31
  600.6 23.6 %shard_map.85 = (f32[128,1024]{1,0:T(8,128)}, bf16[16384,1024]{1,0:T(8,128)(2,1)}) custom-call(s32[25]{0:T(128)} %stack.190.where_ref, bf16[128,8192]{1,0:T(8,128)(2,1)} %get-tuple-element.107.refs_0_, bf16[128,8192]{1,0:T(8,128)(2,1)} %get-tuple-element.105.refs_1_.refs_0_, ...), custom_call_target="tpu_custom_call", output_to_operand_aliasing={{1}: (10, {})} | custom-call | tf_op jit(solution)/shard_map/pallas_call | solution.py:146
  624.2 16.5 %collective-permute-done.31.refs_1_ = bf16[2048,1024]{1,0:T(8,128)(2,1)} collective-permute-done((bf16[2048,1024]{1,0:T(8,128)(2,1)}, bf16[2048,1024]{1,0:T(8,128)(2,1)}, u32[]{:S(2)}, u32[]{:S(2)}) %collective-permute-start.31) | collective-permute-done | bytes 4194336 | tf_op jit(solution)/shard_map/ppermute | solution.py:251
  640.7 6.4 collective-permute-done.32.refs_2_
  647.1 8.7 %shard_map.86 = (f32[128,1024]{1,0:T(8,128)}, bf16[16384,1024]{1,0:T(8,128)(2,1)}) custom-call(s32[10]{0:T(128)} %stack.72.where_ref, bf16[128,8192]{1,0:T(8,128)(2,1)} %get-tuple-element.105.refs_1_.refs_0_, bf16[2048,1024]{1,0:T(8,128)(2,1)} %collective-permute-done.31.refs_1_, ...), custom_call_target="tpu_custom_call", output_to_operand_aliasing={{1}: (5, {})} | custom-call | tf_op jit(solution)/shard_map/pallas_call | solution.py:146
  655.8 2.9 shard_map.87
  (69 shorter events, 17.3 us)
Async XLA Ops:
  1.3 10.3 %copy-start = (bf16[1,128,8192]{2,1,0:T(8,128)(2,1)S(1)}, bf16[1,128,8192]{2,1,0:T(8,128)(2,1)}, u32[]{:S(2)}) copy-start(bf16[1,128,8192]{2,1,0:T(8,128)(2,1)} %param.6) | copy-start | bytes 6291460
  1.3 15.7 %copy-start.5 = (bf16[1,8192]{1,0:T(2,128)(2,1)S(1)}, bf16[1,8192]{1,0:T(2,128)(2,1)}, u32[]{:S(2)}) copy-start(bf16[1,8192]{1,0:T(2,128)(2,1)} %param.7) | copy-start | bytes 49156
  12.2 6.4 collective-permute-start.2
  20.4 19.2 %collective-permute-start.5 = (bf16[128,2048]{1,0:T(8,128)(2,1)}, bf16[128,2048]{1,0:T(8,128)(2,1)}, u32[]{:S(2)}, u32[]{:S(2)}) collective-permute-start(bf16[128,2048]{1,0:T(8,128)(2,1)} %get-tuple-element.127), channel_id=1, source_target_pairs={{0,3},{1,2},{2,1},{3,0},{4,7},{5,6},{6,5},{7,4}} | collective-permute-start | bytes 1572872 | tf_op jit(solution)/shard_map/ppermute | solution.py:251
  26.4 79.6 %collective-permute-start.4 = (bf16[128,2048]{1,0:T(8,128)(2,1)}, bf16[128,2048]{1,0:T(8,128)(2,1)}, u32[]{:S(2)}, u32[]{:S(2)}) collective-permute-start(bf16[128,2048]{1,0:T(8,128)(2,1)} %get-tuple-element.128), channel_id=1, source_target_pairs={{0,2},{1,3},{2,0},{3,1},{4,6},{5,7},{6,4},{7,5}} | collective-permute-start | bytes 1572872 | tf_op jit(solution)/shard_map/ppermute | solution.py:251
  28.3 77.6 %collective-permute-start.3 = (bf16[128,2048]{1,0:T(8,128)(2,1)S(1)}, bf16[128,2048]{1,0:T(8,128)(2,1)}, u32[]{:S(2)}, u32[]{:S(2)}) collective-permute-start(bf16[128,2048]{1,0:T(8,128)(2,1)S(1)} %get-tuple-element.129), channel_id=1, source_target_pairs={{0,1},{1,0},{2,3},{3,2},{4,5},{5,4},{6,7},{7,6}} | collective-permute-start | bytes 1572872 | tf_op jit(solution)/shard_map/ppermute | solution.py:251
  30.8 236.4 %collective-permute-start.1 = (bf16[2048,1024]{1,0:T(8,128)(2,1)}, bf16[2048,1024]{1,0:T(8,128)(2,1)}, u32[]{:S(2)}, u32[]{:S(2)}) collective-permute-start(bf16[2048,1024]{1,0:T(8,128)(2,1)} %get-tuple-element.108.refs_1_.refs_2_), channel_id=1, source_target_pairs={{8,11},{9,10},{10,9},{11,8},{16,19},{17,18},{18,17},{19,16},{12,15... | collective-permute-start | bytes 12582920 | tf_op jit(solution)/shard_map/ppermute | solution.py:251
  33.4 233.8 %collective-permute-start = (bf16[2048,1024]{1,0:T(8,128)(2,1)}, bf16[2048,1024]{1,0:T(8,128)(2,1)}, u32[]{:S(2)}, u32[]{:S(2)}) collective-permute-start(bf16[2048,1024]{1,0:T(8,128)(2,1)} %get-tuple-element.108.refs_1_.refs_2_), channel_id=1, source_target_pairs={{8,9},{9,8},{10,11},{11,10},{16,17},{17,16},{18,19},{19,18},{12,13... | collective-permute-start | bytes 12582920 | tf_op jit(solution)/shard_map/ppermute | solution.py:251
  123.1 149.5 %collective-permute-start.13 = (bf16[2048,1024]{1,0:T(8,128)(2,1)}, bf16[2048,1024]{1,0:T(8,128)(2,1)}, u32[]{:S(2)}, u32[]{:S(2)}) collective-permute-start(bf16[2048,1024]{1,0:T(8,128)(2,1)} %get-tuple-element.84.refs_1_), channel_id=1, source_target_pairs={{8,12},{12,8},{16,20},{20,16},{9,13},{13,9},{17,21},{21,17},{10,14... | collective-permute-start | bytes 12582920 | tf_op jit(solution)/shard_map/ppermute | solution.py:251
  125.7 28.1 %collective-permute-start.6 = (f32[512,1024]{1,0:T(8,128)}, f32[512,1024]{1,0:T(8,128)S(1)}, u32[]{:S(2)}, u32[]{:S(2)}) collective-permute-start(f32[512,1024]{1,0:T(8,128)} %shard_map.79), channel_id=1, source_target_pairs={{0,4},{4,0},{1,5},{5,1},{2,6},{6,2},{3,7},{7,3}} | collective-permute-start | bytes 6291464 | tf_op jit(solution)/shard_map/ppermute | solution.py:251
  157.3 16.4 %copy-start.6 = (s32[1,128]{1,0:T(1,128)S(1)}, s32[1,128]{1,0:T(1,128)}, u32[]{:S(2)}) copy-start(s32[1,128]{1,0:T(1,128)} %param.11) | copy-start | bytes 1540
  157.4 11.1 %collective-permute-start.7 = (bf16[128,1024]{1,0:T(8,128)(2,1)S(1)}, bf16[128,1024]{1,0:T(8,128)(2,1)S(1)}, u32[]{:S(2)}, u32[]{:S(2)}) collective-permute-start(bf16[128,1024]{1,0:T(8,128)(2,1)S(1)} %get-tuple-element.130), channel_id=1, source_target_pairs={{0,1},{1,0},{2,3},{3,2},{4,5},{5,4},{6,7},{7,6}} | collective-permute-start | bytes 786440 | tf_op jit(solution)/shard_map/ppermute | solution.py:251
  159.4 15.9 %collective-permute-start.9 = (bf16[128,1024]{1,0:T(8,128)(2,1)S(1)}, bf16[128,1024]{1,0:T(8,128)(2,1)S(1)}, u32[]{:S(2)}, u32[]{:S(2)}) collective-permute-start(bf16[128,1024]{1,0:T(8,128)(2,1)S(1)} %get-tuple-element.131), channel_id=1, source_target_pairs={{0,3},{1,2},{2,1},{3,0},{4,7},{5,6},{6,5},{7,4}} | collective-permute-start | bytes 786440 | tf_op jit(solution)/shard_map/ppermute | solution.py:251
  168.5 83.8 %collective-permute-start.8 = (bf16[128,1024]{1,0:T(8,128)(2,1)S(1)}, bf16[128,1024]{1,0:T(8,128)(2,1)S(1)}, u32[]{:S(2)}, u32[]{:S(2)}) collective-permute-start(bf16[128,1024]{1,0:T(8,128)(2,1)S(1)} %get-tuple-element.132), channel_id=1, source_target_pairs={{0,2},{1,3},{2,0},{3,1},{4,6},{5,7},{6,4},{7,5}} | collective-permute-start | bytes 786440 | tf_op jit(solution)/shard_map/ppermute | solution.py:251
  175.2 92.0 %collective-permute-start.10 = (bf16[1,8192]{1,0:T(2,128)(2,1)S(1)}, bf16[1,8192]{1,0:T(2,128)(2,1)S(1)}, u32[]{:S(2)}, u32[]{:S(2)}) collective-permute-start(bf16[1,8192]{1,0:T(2,128)(2,1)S(1)} %copy-done.5), channel_id=1, source_target_pairs={{0,4},{4,0},{8,12},{12,8},{16,20},{20,16},{24,28},{28,24},{1,5},{5... | collective-permute-start | bytes 49160 | tf_op jit(solution)/shard_map/ppermute | solution.py:251
  267.2 10.6 %collective-permute-start.11 = (bf16[2048,1024]{1,0:T(8,128)(2,1)}, bf16[2048,1024]{1,0:T(8,128)(2,1)}, u32[]{:S(2)}, u32[]{:S(2)}) collective-permute-start(bf16[2048,1024]{1,0:T(8,128)(2,1)} %get-tuple-element.108.refs_1_.refs_2_), channel_id=1, source_target_pairs={{8,10},{11,9},{16,18},{19,17},{12,14},{15,13},{20,22},{23,21}} | collective-permute-start | bytes 12582920 | tf_op jit(solution)/shard_map/ppermute | solution.py:251
  270.0 7.9 %collective-permute-start.12 = (bf16[2048,1024]{1,0:T(8,128)(2,1)}, bf16[2048,1024]{1,0:T(8,128)(2,1)}, u32[]{:S(2)}, u32[]{:S(2)}) collective-permute-start(bf16[2048,1024]{1,0:T(8,128)(2,1)} %collective-permute-done.1.refs_4_), channel_id=1, source_target_pairs={{10,11},{9,8},{18,19},{17,16},{14,15},{13,12},{22,23},{21,20}} | collective-permute-start | bytes 12582920 | tf_op jit(solution)/shard_map/ppermute | solution.py:251
  272.6 5.2 collective-permute-start.15
  275.3 2.6 collective-permute-start.14
  277.9 48.6 %collective-permute-start.21 = (bf16[2048,1024]{1,0:T(8,128)(2,1)}, bf16[2048,1024]{1,0:T(8,128)(2,1)}, u32[]{:S(2)}, u32[]{:S(2)}) collective-permute-start(bf16[2048,1024]{1,0:T(8,128)(2,1)} %collective-permute-done.13.refs_7_), channel_id=1, source_target_pairs={{8,10},{11,9},{16,18},{19,17},{12,14},{15,13},{20,22},{23,21}} | collective-permute-start | bytes 12582920 | tf_op jit(solution)/shard_map/ppermute | solution.py:251
  280.6 45.8 %collective-permute-start.22 = (bf16[2048,1024]{1,0:T(8,128)(2,1)}, bf16[2048,1024]{1,0:T(8,128)(2,1)}, u32[]{:S(2)}, u32[]{:S(2)}) collective-permute-start(bf16[2048,1024]{1,0:T(8,128)(2,1)} %collective-permute-done.15.refs_9_), channel_id=1, source_target_pairs={{10,11},{9,8},{18,19},{17,16},{14,15},{13,12},{22,23},{21,20}} | collective-permute-start | bytes 12582920 | tf_op jit(solution)/shard_map/ppermute | solution.py:251
  283.9 15.4 %collective-permute-start.16 = (bf16[16,128]{1,0:T(8,128)(2,1)S(1)}, bf16[16,128]{1,0:T(8,128)(2,1)S(1)}, u32[]{:S(2)}, u32[]{:S(2)}) collective-permute-start(bf16[16,128]{1,0:T(8,128)(2,1)S(1)} %slice.29), channel_id=1, source_target_pairs={{8,0},{9,1},{10,2},{11,3},{16,24},{17,25},{18,26},{19,27},{12,4},{... | collective-permute-start | bytes 12296 | tf_op jit(solution)/shard_map/ppermute | solution.py:251
  299.4 27.0 %collective-permute-start.20 = (bf16[128,8192]{1,0:T(8,128)(2,1)}, bf16[128,8192]{1,0:T(8,128)(2,1)}, u32[]{:S(2)}, u32[]{:S(2)}) collective-permute-start(bf16[128,8192]{1,0:T(8,128)(2,1)} %shard_map.80.held_ref), channel_id=1, source_target_pairs={{0,12},{4,8},{1,13},{5,9},{2,14},{6,10},{3,15},{7,11}} | collective-permute-start | bytes 6291464 | tf_op jit(solution)/shard_map/ppermute | solution.py:251
  304.0 22.5 %collective-permute-start.19 = (bf16[128,8192]{1,0:T(8,128)(2,1)}, bf16[128,8192]{1,0:T(8,128)(2,1)S(1)}, u32[]{:S(2)}, u32[]{:S(2)}) collective-permute-start(bf16[128,8192]{1,0:T(8,128)(2,1)} %shard_map.80.held_ref), channel_id=1, source_target_pairs={{0,8},{4,12},{1,9},{5,13},{2,10},{6,14},{3,11},{7,15}} | collective-permute-start | bytes 6291464 | tf_op jit(solution)/shard_map/ppermute | solution.py:251
  326.4 8.0 %copy-start.1 = (bf16[128,8192]{1,0:T(8,128)(2,1)}, bf16[128,8192]{1,0:T(8,128)(2,1)S(1)}, u32[]{:S(2)}) copy-start(bf16[128,8192]{1,0:T(8,128)(2,1)S(1)} %collective-permute-done.19.x_ref) | copy-start | bytes 6291460
  345.5 15.3 %collective-permute-start.25 = (bf16[128,8192]{1,0:T(8,128)(2,1)}, bf16[128,8192]{1,0:T(8,128)(2,1)}, u32[]{:S(2)}, u32[]{:S(2)}) collective-permute-start(bf16[128,8192]{1,0:T(8,128)(2,1)} %shard_map.82.held_ref), channel_id=1, source_target_pairs={{8,20},{12,16},{9,21},{13,17},{10,22},{14,18},{11,23},{15,19}} | collective-permute-start | bytes 6291464 | tf_op jit(solution)/shard_map/ppermute | solution.py:251
  347.4 15.4 %collective-permute-start.24 = (bf16[128,8192]{1,0:T(8,128)(2,1)}, bf16[128,8192]{1,0:T(8,128)(2,1)S(1)}, u32[]{:S(2)}, u32[]{:S(2)}) collective-permute-start(bf16[128,8192]{1,0:T(8,128)(2,1)} %shard_map.82.held_ref), channel_id=1, source_target_pairs={{8,16},{12,20},{9,17},{13,21},{10,18},{14,22},{11,19},{15,23}} | collective-permute-start | bytes 6291464 | tf_op jit(solution)/shard_map/ppermute | solution.py:251
  348.2 52.7 %collective-permute-start.18 = (bf16[2048,1024]{1,0:T(8,128)(2,1)}, bf16[2048,1024]{1,0:T(8,128)(2,1)}, u32[]{:S(2)}, u32[]{:S(2)}) collective-permute-start(bf16[2048,1024]{1,0:T(8,128)(2,1)} %get-tuple-element.108.refs_1_.refs_2_), channel_id=1, source_target_pairs={{0,3},{1,2},{2,1},{3,0},{24,27},{25,26},{26,25},{27,24},{4,7},{5,6... | collective-permute-start | bytes 12582920 | tf_op jit(solution)/shard_map/ppermute | solution.py:251
  352.3 93.5 %collective-permute-start.17 = (bf16[2048,1024]{1,0:T(8,128)(2,1)}, bf16[2048,1024]{1,0:T(8,128)(2,1)}, u32[]{:S(2)}, u32[]{:S(2)}) collective-permute-start(bf16[2048,1024]{1,0:T(8,128)(2,1)} %get-tuple-element.108.refs_1_.refs_2_), channel_id=1, source_target_pairs={{0,1},{1,0},{2,3},{3,2},{24,25},{25,24},{26,27},{27,26},{4,5},{5,4... | collective-permute-start | bytes 12582920 | tf_op jit(solution)/shard_map/ppermute | solution.py:251
  357.7 88.1 %collective-permute-start.23 = (bf16[2048,1024]{1,0:T(8,128)(2,1)}, bf16[2048,1024]{1,0:T(8,128)(2,1)}, u32[]{:S(2)}, u32[]{:S(2)}) collective-permute-start(bf16[2048,1024]{1,0:T(8,128)(2,1)} %get-tuple-element.84.refs_1_), channel_id=1, source_target_pairs={{0,4},{4,0},{24,28},{28,24},{1,5},{5,1},{25,29},{29,25},{2,6},{6,2... | collective-permute-start | bytes 12582920 | tf_op jit(solution)/shard_map/ppermute | solution.py:251
  362.9 5.5 copy-start.3
  445.8 13.5 %collective-permute-start.30 = (bf16[128,8192]{1,0:T(8,128)(2,1)}, bf16[128,8192]{1,0:T(8,128)(2,1)S(1)}, u32[]{:S(2)}, u32[]{:S(2)}) collective-permute-start(bf16[128,8192]{1,0:T(8,128)(2,1)} %shard_map.84.held_ref), channel_id=1, source_target_pairs={{16,28},{20,24},{17,29},{21,25},{18,30},{22,26},{19,31},{23,27}} | collective-permute-start | bytes 6291464 | tf_op jit(solution)/shard_map/ppermute | solution.py:251
  446.6 13.2 %collective-permute-start.29 = (bf16[128,8192]{1,0:T(8,128)(2,1)}, bf16[128,8192]{1,0:T(8,128)(2,1)S(1)}, u32[]{:S(2)}, u32[]{:S(2)}) collective-permute-start(bf16[128,8192]{1,0:T(8,128)(2,1)} %shard_map.84.held_ref), channel_id=1, source_target_pairs={{16,24},{20,28},{17,25},{21,29},{18,26},{22,30},{19,27},{23,31}} | collective-permute-start | bytes 6291464 | tf_op jit(solution)/shard_map/ppermute | solution.py:251
  450.0 50.4 %collective-permute-start.26 = (bf16[2048,1024]{1,0:T(8,128)(2,1)S(1)}, bf16[2048,1024]{1,0:T(8,128)(2,1)S(1)}, u32[]{:S(2)}, u32[]{:S(2)}) collective-permute-start(bf16[2048,1024]{1,0:T(8,128)(2,1)S(1)} %broadcast_select_fusion), channel_id=1, source_target_pairs={{0,2},{1,0},{2,3},{3,1},{24,26},{25,24},{26,27},{27,25},{4,6},{5,4... | collective-permute-start | bytes 12582920 | tf_op jit(solution)/shard_map/ppermute | solution.py:251
  453.3 93.1 %collective-permute-start.28 = (bf16[2048,1024]{1,0:T(8,128)(2,1)}, bf16[2048,1024]{1,0:T(8,128)(2,1)}, u32[]{:S(2)}, u32[]{:S(2)}) collective-permute-start(bf16[2048,1024]{1,0:T(8,128)(2,1)} %collective-permute-done.23.refs_6_), channel_id=1, source_target_pairs={{0,3},{1,2},{2,1},{3,0},{24,27},{25,26},{26,25},{27,24},{4,7},{5,6... | collective-permute-start | bytes 12582920 | tf_op jit(solution)/shard_map/ppermute | solution.py:251
  456.9 133.5 %collective-permute-start.27 = (bf16[2048,1024]{1,0:T(8,128)(2,1)}, bf16[2048,1024]{1,0:T(8,128)(2,1)}, u32[]{:S(2)}, u32[]{:S(2)}) collective-permute-start(bf16[2048,1024]{1,0:T(8,128)(2,1)} %collective-permute-done.23.refs_6_), channel_id=1, source_target_pairs={{0,1},{1,0},{2,3},{3,2},{24,25},{25,24},{26,27},{27,26},{4,5},{5,4... | collective-permute-start | bytes 12582920 | tf_op jit(solution)/shard_map/ppermute | solution.py:251
  459.8 3.6 copy-start.2
  500.4 2.1 copy-start.4
  590.4 50.3 %collective-permute-start.31 = (bf16[2048,1024]{1,0:T(8,128)(2,1)}, bf16[2048,1024]{1,0:T(8,128)(2,1)}, u32[]{:S(2)}, u32[]{:S(2)}) collective-permute-start(bf16[2048,1024]{1,0:T(8,128)(2,1)} %collective-permute-done.23.refs_6_), channel_id=1, source_target_pairs={{0,2},{3,1},{24,26},{27,25},{4,6},{7,5},{28,30},{31,29}} | collective-permute-start | bytes 12582920 | tf_op jit(solution)/shard_map/ppermute | solution.py:251
  596.4 50.7 %collective-permute-start.32 = (bf16[2048,1024]{1,0:T(8,128)(2,1)}, bf16[2048,1024]{1,0:T(8,128)(2,1)}, u32[]{:S(2)}, u32[]{:S(2)}) collective-permute-start(bf16[2048,1024]{1,0:T(8,128)(2,1)} %collective-permute-done.28.refs_8_), channel_id=1, source_target_pairs={{2,3},{1,0},{26,27},{25,24},{6,7},{5,4},{30,31},{29,28}} | collective-permute-start | bytes 12582920 | tf_op jit(solution)/shard_map/ppermute | solution.py:251
